TPU v7x, 128 devices: a whole 4x4x4 slice. The times are simulated.
128 devices in a mesh: grp: 64 (over z_hi, y, x, core), seq: 2 (over z_lo).
Axes of the slice: x: 4, y: 4, z: 4 (z_hi: 2, z_lo: 2; z = z_hi * 2 + z_lo), core: 2. Of those that a mesh axis runs over, the one named last changes fastest.
Arguments:
- tokens: bfloat16 [32768, 768], P(('grp', 'seq')), may hold values from -6 to 6
- w_qkv: bfloat16 [768, 2304], P(('grp', 'seq')), may hold values from -0.21875 to 0.21875
- w_out: bfloat16 [768, 768], P(('grp', 'seq')), may hold values from -2.5 to 2.5
- w_up: bfloat16 [768, 3072], P(('grp', 'seq')), may hold values from -0.21875 to 0.21875
- w_down: bfloat16 [3072, 768], P(('grp', 'seq')), may hold values from -0.109375 to 0.109375
- gain_attn: bfloat16 [768], P(('grp', 'seq')), may hold values from 0.099609375 to 1.8984375
- gain_ffn: bfloat16 [768], P(('grp', 'seq')), may hold values from 0.099609375 to 1.8984375
- conv_taps: bfloat16 [3, 2304], P(None, ('grp', 'seq')), may hold values from -1 to 1
- cotangent: bfloat16 [32768, 768], P(('grp', 'seq')), may hold values from -6 to 6
Outputs:
- output: bfloat16 [32768, 768], P(('grp', 'seq'))
- grad_tokens: bfloat16 [32768, 768], P(('grp', 'seq'))
- grad_w_qkv: float32 [768, 2304], P(('grp', 'seq'))
- grad_w_out: float32 [768, 768], P(('grp', 'seq'))
- grad_w_up: float32 [768, 3072], P(('grp', 'seq'))
- grad_w_down: float32 [3072, 768], P(('grp', 'seq'))
- grad_gain_attn: float32 [768], P(('grp', 'seq'))
- grad_gain_ffn: float32 [768], P(('grp', 'seq'))
- grad_conv_taps: float32 [3, 2304], P(None, ('grp', 'seq'))
All inputs are finite; a program needn't handle non-finite values.
Results may differ from a plain program's by a relative error of at most 0.017.
Values may be sent and summed in bfloat16 or wider, within the bound.
A program may use at most 128 MiB of HBM per device.

v0:
```python
import jax
import jax.numpy as jnp
from jax import lax
from jax.sharding import PartitionSpec as P

HEAD_DIM = 64


epsilon = 1e-05


def normalize(values):
    mean = jnp.mean(values, axis=-1, keepdims=True)
    centred = values - mean
    inverse = lax.rsqrt(jnp.mean(centred * centred, axis=-1, keepdims=True) + epsilon)
    return (centred * inverse, inverse)


def norm_back(grad_normed, normed, inverse):
    first = jnp.mean(grad_normed, axis=-1, keepdims=True)
    second = jnp.mean(grad_normed * normed, axis=-1, keepdims=True)
    return inverse * (grad_normed - first - normed * second)


def delayed(values, steps):
    padding = jnp.zeros((steps,) + values.shape[1:], values.dtype)
    return jnp.concatenate([padding, values[: values.shape[0] - steps]], axis=0)


def advanced(values, steps):
    padding = jnp.zeros((steps,) + values.shape[1:], values.dtype)
    return jnp.concatenate([values[steps:], padding], axis=0)


def causal_mask(length):
    rows = lax.broadcasted_iota(jnp.int32, (length, length), 0)
    columns = lax.broadcasted_iota(jnp.int32, (length, length), 1)
    return columns <= rows


def head_scores(query, key):
    scores = jnp.einsum("qd,kd->qk", query, key, preferred_element_type=jnp.float32) * HEAD_DIM ** (
        -0.5
    )
    return jnp.where(causal_mask(query.shape[0]), scores, -1e30)


def head_forward(operands):
    query, key, value = operands
    masked = head_scores(query, key)
    top = jnp.max(masked, axis=-1, keepdims=True)
    weights = jnp.exp(masked - top)
    total = jnp.sum(weights, axis=-1, keepdims=True)
    probs = (weights / total).astype(jnp.bfloat16)
    result = jnp.dot(probs, value, preferred_element_type=jnp.float32).astype(jnp.bfloat16)
    return (result, top[:, 0] + jnp.log(total[:, 0]))


def head_backward(operands):
    query, key, value, grad_out, log_total = operands
    masked = head_scores(query, key)
    exact = jnp.exp(masked - log_total[:, None])
    probs = exact.astype(jnp.bfloat16)
    grad_value = jnp.einsum("qk,qd->kd", probs, grad_out, preferred_element_type=jnp.float32)
    grad_probs = jnp.einsum("qd,kd->qk", grad_out, value, preferred_element_type=jnp.float32)
    centred = grad_probs - jnp.sum(grad_probs * exact, axis=-1, keepdims=True)
    grad_scores = (exact * centred).astype(jnp.bfloat16)
    grad_query = jnp.dot(grad_scores, key, preferred_element_type=jnp.float32) * HEAD_DIM ** (-0.5)
    grad_key = jnp.einsum(
        "qk,qd->kd", grad_scores, query, preferred_element_type=jnp.float32
    ) * HEAD_DIM ** (-0.5)
    return (grad_query, grad_key, grad_value)


def contract_rows(left, right):
    return lax.dot_general(
        left, right, (((0,), (0,)), ((), ())), preferred_element_type=jnp.float32
    )


def per_device(tokens, w_qkv, w_out, w_up, w_down, gain_attn, gain_ffn, conv_taps, cotangent):
    shards = (w_qkv, w_out, w_up, w_down, gain_attn, gain_ffn, conv_taps)
    full = (
        lax.all_gather(shards[0], ("grp", "seq"), axis=0, tiled=True),
        lax.all_gather(shards[1], ("grp", "seq"), axis=0, tiled=True),
        lax.all_gather(shards[2], ("grp", "seq"), axis=0, tiled=True),
        lax.all_gather(shards[3], ("grp", "seq"), axis=0, tiled=True),
        lax.all_gather(shards[4], ("grp", "seq"), axis=0, tiled=True),
        lax.all_gather(shards[5], ("grp", "seq"), axis=0, tiled=True),
        lax.all_gather(shards[6], ("grp", "seq"), axis=1, tiled=True),
    )
    weight_qkv, weight_out, weight_up, weight_down, full_gain_attn, full_gain_ffn, full_taps = full
    tok_rows, width = tokens.shape
    groups = lax.axis_size("seq")
    part = width // groups
    local_heads = part // HEAD_DIM
    rank = lax.axis_index("seq")
    inputs = tokens.astype(jnp.float32)
    gain_one = full_gain_attn.astype(jnp.float32)
    gain_two = full_gain_ffn.astype(jnp.float32)
    taps_all = full_taps.astype(jnp.float32).reshape(3, 3, width)
    local_taps = lax.dynamic_slice_in_dim(taps_all, rank * part, part, 2)
    normed_one, inverse_one = normalize(inputs)
    hidden_one = (normed_one * gain_one).astype(jnp.bfloat16)
    qkv = jnp.dot(hidden_one, weight_qkv, preferred_element_type=jnp.float32).astype(jnp.bfloat16)
    heads_in = lax.all_to_all(
        qkv.reshape(tok_rows, 3, width), "seq", split_axis=2, concat_axis=0, tiled=True
    )
    length = heads_in.shape[0]
    raw_values = heads_in.astype(jnp.float32)
    conv_out = (
        local_taps[0] * raw_values
        + local_taps[1] * delayed(raw_values, 1)
        + local_taps[2] * delayed(raw_values, 2)
    )
    mixed = conv_out.astype(jnp.bfloat16)

    def per_head(block):
        return block.reshape(length, local_heads, HEAD_DIM).transpose(1, 0, 2)

    query = per_head(mixed[:, 0])
    key = per_head(mixed[:, 1])
    value = per_head(mixed[:, 2])
    head_out, log_total = lax.map(head_forward, (query, key, value))
    head_rows = head_out.transpose(1, 0, 2).reshape(length, part)
    attended = lax.all_to_all(head_rows, "seq", split_axis=0, concat_axis=1, tiled=True)
    resid = inputs + jnp.dot(attended, weight_out, preferred_element_type=jnp.float32)
    normed_two, inverse_two = normalize(resid)
    hidden_two = (normed_two * gain_two).astype(jnp.bfloat16)
    up_proj = jnp.dot(hidden_two, weight_up, preferred_element_type=jnp.float32)
    rectified = jax.nn.relu(up_proj)
    act = (rectified * rectified).astype(jnp.bfloat16)
    output = (resid + jnp.dot(act, weight_down, preferred_element_type=jnp.float32)).astype(
        jnp.bfloat16
    )
    grad_out = cotangent.astype(jnp.float32)
    grad_w_down = contract_rows(act, cotangent)
    grad_act = jnp.dot(cotangent, weight_down.T, preferred_element_type=jnp.float32)
    grad_up = (grad_act * 2.0 * rectified).astype(jnp.bfloat16)
    grad_w_up = contract_rows(hidden_two, grad_up)
    grad_hidden_two = jnp.dot(grad_up, weight_up.T, preferred_element_type=jnp.float32)
    grad_gain_ffn = jnp.sum(grad_hidden_two * normed_two, axis=0)
    grad_resid = grad_out + norm_back(grad_hidden_two * gain_two, normed_two, inverse_two)
    grad_proj = grad_resid.astype(jnp.bfloat16)
    grad_w_out = contract_rows(attended, grad_proj)
    grad_attended = jnp.dot(grad_proj, weight_out.T, preferred_element_type=jnp.float32).astype(
        jnp.bfloat16
    )
    grad_heads = lax.all_to_all(grad_attended, "seq", split_axis=1, concat_axis=0, tiled=True)
    grad_query, grad_key, grad_value = lax.map(
        head_backward, (query, key, value, per_head(grad_heads), log_total)
    )

    def to_rows(block):
        return block.transpose(1, 0, 2).reshape(length, part)

    grad_mixed = jnp.stack([to_rows(grad_query), to_rows(grad_key), to_rows(grad_value)], axis=1)
    grad_raw = (
        local_taps[0] * grad_mixed
        + local_taps[1] * advanced(grad_mixed, 1)
        + local_taps[2] * advanced(grad_mixed, 2)
    )
    tap_grads = jnp.stack(
        [
            jnp.sum(grad_mixed * raw_values, axis=0),
            jnp.sum(grad_mixed * delayed(raw_values, 1), axis=0),
            jnp.sum(grad_mixed * delayed(raw_values, 2), axis=0),
        ]
    )
    taps_holder = jnp.zeros((3, 3, width), jnp.float32)
    grad_taps = lax.dynamic_update_slice_in_dim(taps_holder, tap_grads, rank * part, 2).reshape(
        3, 3 * width
    )
    grad_qkv = lax.all_to_all(
        grad_raw.astype(jnp.bfloat16), "seq", split_axis=0, concat_axis=2, tiled=True
    ).reshape(tok_rows, 3 * width)
    grad_w_qkv = contract_rows(hidden_one, grad_qkv)
    grad_hidden_one = jnp.dot(grad_qkv, weight_qkv.T, preferred_element_type=jnp.float32)
    grad_gain_attn = jnp.sum(grad_hidden_one * normed_one, axis=0)
    grad_tokens = (
        grad_resid + norm_back(grad_hidden_one * gain_one, normed_one, inverse_one)
    ).astype(jnp.bfloat16)
    terms = (
        grad_w_qkv,
        grad_w_out,
        grad_w_up,
        grad_w_down,
        grad_gain_attn,
        grad_gain_ffn,
        grad_taps,
    )
    summed = (
        lax.psum_scatter(terms[0], ("grp", "seq"), scatter_dimension=0, tiled=True),
        lax.psum_scatter(terms[1], ("grp", "seq"), scatter_dimension=0, tiled=True),
        lax.psum_scatter(terms[2], ("grp", "seq"), scatter_dimension=0, tiled=True),
        lax.psum_scatter(terms[3], ("grp", "seq"), scatter_dimension=0, tiled=True),
        lax.psum_scatter(terms[4], ("grp", "seq"), scatter_dimension=0, tiled=True),
        lax.psum_scatter(terms[5], ("grp", "seq"), scatter_dimension=0, tiled=True),
        lax.psum_scatter(terms[6], ("grp", "seq"), scatter_dimension=1, tiled=True),
    )
    return (output, grad_tokens) + tuple(summed)


def solution(mesh):
    placed = (
        P(("grp", "seq"), None),
        P(("grp", "seq"), None),
        P(("grp", "seq"), None),
        P(("grp", "seq"), None),
        P(("grp", "seq"), None),
        P(("grp", "seq")),
        P(("grp", "seq")),
        P(None, ("grp", "seq")),
        P(("grp", "seq"), None),
    )
    return jax.shard_map(
        per_device,
        mesh=mesh,
        in_specs=placed,
        out_specs=(
            P(("grp", "seq"), None),
            P(("grp", "seq"), None),
            P(("grp", "seq"), None),
            P(("grp", "seq"), None),
            P(("grp", "seq"), None),
            P(("grp", "seq"), None),
            P(("grp", "seq")),
            P(("grp", "seq")),
            P(None, ("grp", "seq")),
        ),
        check_vma=False,
    )
```

profile of v0, /device:TPU:1, one launch (start us, length us, event | category | flops | bytes accessed | tf_op | source)
XLA Modules:
  0.0 2550.8 jit_solution(1656630467792107986)
XLA Ops:
  11.7 68.7 %all-reduce.16 = (bf16[768]{0:T(1024)(128)(2,1)S(1)}, bf16[768]{0:T(1024)(128)(2,1)}) all-reduce(bf16[768]{0:T(1024)(128)(2,1)S(1)} %dynamic-update-slice, bf16[768]{0:T(1024)(128)(2,1)S(1)} %dynamic-update-slice.1), channel_id=1, replica_groups=mesh['grp'=64,'seq'=2] {'grp','seq'}, use_global_device_ids=true, to_apply=%add.4 | all-reduce | flops 1536 | bytes 6144
  82.8 238.4 %all-gather.11.cloned.1.call-done = bf16[128,6,2304]{2,1,0:T(8,128)(2,1)} async-done(((bf16[1,6,2304]{2,1,0:T(8,128)(2,1)}), bf16[128,6,2304]{2,1,0:T(8,128)(2,1)}) %all-gather.11.cloned.1.call-update) | async-done | bytes 3538960 | tf_op jit(solution)/shard_map/all_gather | solution.py:84
  321.2 6.6 reshape.139
  337.5 320.3 %all-gather = bf16[128,18,3]{1,2,0:T(4,128)(2,1)S(1)} all-gather(bf16[1,18,3]{1,2,0:T(4,128)(2,1)S(1)} %bitcast.216), channel_id=1, replica_groups=mesh['grp'=64,'seq'=2] {'grp','seq'}, dimensions={0}, use_global_device_ids=true | all-gather | bytes 13932 | tf_op jit(solution)/shard_map/all_gather | solution.py:90
  674.5 22.8 while.26
  713.7 219.5 %all-gather.15.cloned.1.call-done = bf16[128,6,3072]{2,1,0:T(8,128)(2,1)} async-done(((bf16[1,6,3072]{2,1,0:T(8,128)(2,1)}), bf16[128,6,3072]{2,1,0:T(8,128)(2,1)}) %all-gather.15.cloned.1.call-update) | async-done | bytes 4718608 | tf_op jit(solution)/shard_map/all_gather | solution.py:86
  933.2 7.7 reshape.143
  946.4 5.0 fusion.62
  951.5 292.5 %all-gather.9.cloned.1.call-done = bf16[3072,768]{1,0:T(8,128)(2,1)} async-done(((bf16[24,768]{1,0:T(8,128)(2,1)}), bf16[3072,768]{1,0:T(8,128)(2,1)}) %all-gather.9.cloned.1.call-update) | async-done | bytes 4718608 | tf_op jit(solution)/shard_map/all_gather | solution.py:87
  1243.9 4.9 fusion.45
  1250.0 5.3 multiply_reduce_fusion.3
  1261.8 4.6 all-to-all-start.2
  1266.4 8.6 all-to-all-done.2
  1279.1 53.5 %while.27 = (s32[]{:T(128)}, f32[6,512,64]{1,2,0:T(8,128)}, f32[6,512,64]{1,2,0:T(8,128)}, f32[6,512,64]{1,2,0:T(8,128)}, bf16[6,512,64]{2,1,0:T(8,128)(2,1)}, /...) while((s32[]{:T(128)}, f32[6,512,64]{1,2,0:T(8,128)}, ...), condition=%wide.region_12.13_spmd, body=%wide.region_10.12_spmd.sunk | while | flops 170458624 | bytes 9059441 | solution.py:150
  1354.4 5.1 fusion.69
  1359.5 15.9 all-to-all-done.3
  1379.2 4.2 fusion.66
  1383.4 704.5 %fusion.70 = (f32[8,2304]{1,0:T(8,128)}, f32[8,768]{1,0:T(8,128)}, f32[8,3072]{1,0:T(8,128)}) fusion(f32[768,2304]{1,0:T(8,128)} %fusion.66, f32[768,768]{1,0:T(8,128)} %fusion.63, f32[768,3072]{1,0:T(8,128)} %fusion.69), kind=kCustom, calls=%all-reduce-scatter.3 | all-reduce-scatter fusion | flops 6291457 | bytes 19070976
  2094.4 10.7 collective-permute-start.60
  2114.4 8.6 collective-permute-start.54
  2170.7 4.2 collective-permute-start.35
  2218.8 5.3 collective-permute-start.18
  2235.5 4.7 fusion.47
  2327.6 65.4 %all-reduce.15 = (f32[768]{0:T(1024)S(1)}, f32[768]{0:T(1024)S(1)}, f32[3,2304]{1,0:T(4,128)S(1)}) all-reduce(f32[768]{0:T(1024)S(1)} %get-tuple-element.190, f32[768]{0:T(1024)S(1)} %copy-done.119, f32[3,2304]{1,0:T(4,128)S(1)} %bitcast.207), channel_id=6, replica_groups=mesh['grp'=64,'seq'=2] {'grp','seq'}, use_global_device_ids=true, to_apply=%region_20.21.clone | all-reduce | flops 8448 | bytes 67584
  2406.9 5.8 collective-permute-start.74
  2413.4 27.2 %concatenate.20 = f32[262,768]{1,0:T(8,128)S(1)} concatenate(f32[6,768]{1,0:T(8,128)} %copy-done.85, f32[8,768]{1,0:T(8,128)} %copy-done.83, f32[8,768]{1,0:T(8,128)} %copy-done.84, f32[8,768]{1,0:T(8,128)} %copy-done.86, f32[8,768]{1,0:T(8,128)} %copy-done.87, f32[8,768]{1,0:T(8,128)} %copy-done.88, f32[8,768]{1,0:T(8,128)} %copy-done.89, f32[8,768]{1,0:T(8,128)} %copy-done.90, ...), dimensions={0} | concatenate | bytes 1609728
  2440.6 4.2 collective-permute-start.73
  2446.8 4.2 collective-permute-start.71
  2454.8 4.9 collective-permute-start.69
  2460.5 33.5 %concatenate.19 = f32[262,2304]{1,0:T(8,128)S(1)} concatenate(f32[6,2304]{1,0:T(8,128)} %copy-done.58, f32[8,2304]{1,0:T(8,128)} %collective-permute-done.30, f32[8,2304]{1,0:T(8,128)} %collective-permute-done.29, f32[8,2304]{1,0:T(8,128)} %collective-permute-done.28, f32[8,2304]{1,0:T(8,128)} %collective-permute-done.27, f32[8,2304]{1,0:T(8,128)} %collective-permute-done.26, ...), dimensions={0} | concatenate | bytes 4829184
  2505.4 4.3 collective-permute-start.64
  2511.9 31.5 %concatenate.21 = f32[262,3072]{1,0:T(8,128)S(1)} concatenate(f32[6,3072]{1,0:T(8,128)S(1)} %copy-done.28, f32[8,3072]{1,0:T(8,128)S(1)} %copy-done.26, f32[8,3072]{1,0:T(8,128)S(1)} %copy-done.30, f32[8,3072]{1,0:T(8,128)} %copy-done.31, f32[8,3072]{1,0:T(8,128)} %copy-done.32, f32[8,3072]{1,0:T(8,128)} %copy-done.33, f32[8,3072]{1,0:T(8,128)} %copy-done.34, ...), dimensions={0} | concatenate | bytes 6438912
  (596 shorter events, 407.5 us)
Async XLA Ops:
  7.2 314.0 %all-gather.11.cloned.1.call-start = ((), (), s32[]{:S(2)}) async-start(), calls=%async_computation.7 | async-start | bytes 4755456 | tf_op jit(solution)/shard_map/all_gather | solution.py:84
  7.9 697.7 %all-gather.13.cloned.1.call-start = ((), (), s32[]{:S(2)}) async-start(), calls=%async_computation.8 | async-start | bytes 1585152 | tf_op jit(solution)/shard_map/all_gather | solution.py:85
  8.7 924.5 %all-gather.15.cloned.1.call-start = ((), (), s32[]{:S(2)}) async-start(), calls=%async_computation.9 | async-start | bytes 6340608 | tf_op jit(solution)/shard_map/all_gather | solution.py:86
  9.4 1234.5 %all-gather.9.cloned.1.call-start = ((), (), s32[]{:S(2)}) async-start(), calls=%async_computation.5 | async-start | bytes 4755456 | tf_op jit(solution)/shard_map/all_gather | solution.py:87
  333.8 324.5 %all-to-all-start = ((bf16[256,3,768]{0,1,2:T(4,128)(2,1)}), bf16[256,3,768]{0,1,2:T(4,128)(2,1)S(1)}, u32[]{:S(2)}, u32[]{:S(2)}) async-start(bf16[256,3,768]{0,1,2:T(4,128)(2,1)} %copy.129), calls=%async_computation | async-start | bytes 3145728 | tf_op jit(solution)/shard_map/all_to_all | solution.py:106
  704.6 1839.4 %reduce-scatter.9.cloned.1.call-start = ((), (), s32[]{:S(2)}) async-start(), calls=%async_computation.6 | async-start | bytes 9510912 | tf_op jit(solution)/shard_map/reduce_scatter | solution.py:196
  1347.6 27.8 %all-to-all-start.3 = ((bf16[512,3,384]{2,1,0:T(4,128)(2,1)}), bf16[512,3,384]{2,1,0:T(4,128)(2,1)S(1)}, u32[]{:S(2)}, u32[]{:S(2)}) async-start(bf16[512,3,384]{2,1,0:T(4,128)(2,1)} %copy.148), calls=%async_computation.3 | async-start | bytes 3145728 | tf_op jit(solution)/shard_map/all_to_all | solution.py:174
  2087.9 22.6 collective-permute-start.62
  2089.2 22.6 collective-permute-start.61
  2176.6 24.4 collective-permute-start.30
  2178.6 24.5 collective-permute-start.29
  2181.3 23.7 collective-permute-start.28
  2224.1 20.9 collective-permute-start.17
  2226.0 21.9 collective-permute-start.16
  2227.9 22.5 collective-permute-start.15
  2229.8 22.8 collective-permute-start.14
  2231.8 24.2 collective-permute-start.13
  2315.0 79.2 %collective-permute-start.83 = (f32[8,3072]{1,0:T(8,128)}, f32[8,3072]{1,0:T(8,128)S(1)}, u32[]{:S(2)}, u32[]{:S(2)}) collective-permute-start(f32[8,3072]{1,0:T(8,128)} %get-tuple-element.234), channel_id=1, source_target_pairs={{0,20},{1,21},{2,22},{3,23},{4,24},{5,25},{6,26},{7,27},{8,28},{9,... | collective-permute-start | bytes 294920
  2317.5 79.8 %collective-permute-start.82 = (f32[8,3072]{1,0:T(8,128)}, f32[8,3072]{1,0:T(8,128)S(1)}, u32[]{:S(2)}, u32[]{:S(2)}) collective-permute-start(f32[8,3072]{1,0:T(8,128)} %get-tuple-element.234), channel_id=1, source_target_pairs={{0,19},{1,20},{2,21},{3,22},{4,23},{5,24},{6,25},{7,26},{8,27},{9,... | collective-permute-start | bytes 294920
  2321.4 78.9 %collective-permute-start.81 = (f32[8,3072]{1,0:T(8,128)}, f32[8,3072]{1,0:T(8,128)S(1)}, u32[]{:S(2)}, u32[]{:S(2)}) collective-permute-start(f32[8,3072]{1,0:T(8,128)} %get-tuple-element.234), channel_id=1, source_target_pairs={{0,18},{1,19},{2,20},{3,21},{4,22},{5,23},{6,24},{7,25},{8,26},{9,... | collective-permute-start | bytes 294920
  2322.7 81.5 %collective-permute-start.80 = (f32[8,3072]{1,0:T(8,128)}, f32[8,3072]{1,0:T(8,128)S(1)}, u32[]{:S(2)}, u32[]{:S(2)}) collective-permute-start(f32[8,3072]{1,0:T(8,128)} %get-tuple-element.234), channel_id=1, source_target_pairs={{0,17},{1,18},{2,19},{3,20},{4,21},{5,22},{6,23},{7,24},{8,25},{9,... | collective-permute-start | bytes 294920
  2325.2 81.6 %collective-permute-start.79 = (f32[8,3072]{1,0:T(8,128)}, f32[8,3072]{1,0:T(8,128)S(1)}, u32[]{:S(2)}, u32[]{:S(2)}) collective-permute-start(f32[8,3072]{1,0:T(8,128)} %get-tuple-element.234), channel_id=1, source_target_pairs={{0,16},{1,17},{2,18},{3,19},{4,20},{5,21},{6,22},{7,23},{8,24},{9,... | collective-permute-start | bytes 294920
  2394.2 46.4 %collective-permute-start.78 = (f32[8,3072]{1,0:T(8,128)}, f32[8,3072]{1,0:T(8,128)S(1)}, u32[]{:S(2)}, u32[]{:S(2)}) collective-permute-start(f32[8,3072]{1,0:T(8,128)} %get-tuple-element.234), channel_id=1, source_target_pairs={{0,15},{1,16},{2,17},{3,18},{4,19},{5,20},{6,21},{7,22},{8,23},{9,... | collective-permute-start | bytes 294920
  2397.3 47.5 %collective-permute-start.77 = (f32[8,3072]{1,0:T(8,128)}, f32[8,3072]{1,0:T(8,128)S(1)}, u32[]{:S(2)}, u32[]{:S(2)}) collective-permute-start(f32[8,3072]{1,0:T(8,128)} %get-tuple-element.234), channel_id=1, source_target_pairs={{0,14},{1,15},{2,16},{3,17},{4,18},{5,19},{6,20},{7,21},{8,22},{9,... | collective-permute-start | bytes 294920
  2400.3 46.5 %collective-permute-start.76 = (f32[8,3072]{1,0:T(8,128)}, f32[8,3072]{1,0:T(8,128)S(1)}, u32[]{:S(2)}, u32[]{:S(2)}) collective-permute-start(f32[8,3072]{1,0:T(8,128)} %get-tuple-element.234), channel_id=1, source_target_pairs={{0,13},{1,14},{2,15},{3,16},{4,17},{5,18},{6,19},{7,20},{8,21},{9,... | collective-permute-start | bytes 294920
  2404.2 46.8 %collective-permute-start.75 = (f32[8,3072]{1,0:T(8,128)}, f32[8,3072]{1,0:T(8,128)S(1)}, u32[]{:S(2)}, u32[]{:S(2)}) collective-permute-start(f32[8,3072]{1,0:T(8,128)} %get-tuple-element.234), channel_id=1, source_target_pairs={{0,12},{1,13},{2,14},{3,15},{4,16},{5,17},{6,18},{7,19},{8,20},{9,... | collective-permute-start | bytes 294920
  2406.9 47.9 %collective-permute-start.74 = (f32[8,3072]{1,0:T(8,128)}, f32[8,3072]{1,0:T(8,128)S(1)}, u32[]{:S(2)}, u32[]{:S(2)}) collective-permute-start(f32[8,3072]{1,0:T(8,128)} %get-tuple-element.234), channel_id=1, source_target_pairs={{0,11},{1,12},{2,13},{3,14},{4,15},{5,16},{6,17},{7,18},{8,19},{9,... | collective-permute-start | bytes 294920
  2440.6 53.5 %collective-permute-start.73 = (f32[8,3072]{1,0:T(8,128)}, f32[8,3072]{1,0:T(8,128)S(1)}, u32[]{:S(2)}, u32[]{:S(2)}) collective-permute-start(f32[8,3072]{1,0:T(8,128)} %get-tuple-element.234), channel_id=1, source_target_pairs={{0,10},{1,11},{2,12},{3,13},{4,14},{5,15},{6,16},{7,17},{8,18},{9,... | collective-permute-start | bytes 294920
  2444.8 52.8 %collective-permute-start.72 = (f32[8,3072]{1,0:T(8,128)}, f32[8,3072]{1,0:T(8,128)S(1)}, u32[]{:S(2)}, u32[]{:S(2)}) collective-permute-start(f32[8,3072]{1,0:T(8,128)} %get-tuple-element.234), channel_id=1, source_target_pairs={{0,9},{1,10},{2,11},{3,12},{4,13},{5,14},{6,15},{7,16},{8,17},{9,1... | collective-permute-start | bytes 294920
  2446.8 54.2 %collective-permute-start.71 = (f32[8,3072]{1,0:T(8,128)}, f32[8,3072]{1,0:T(8,128)S(1)}, u32[]{:S(2)}, u32[]{:S(2)}) collective-permute-start(f32[8,3072]{1,0:T(8,128)} %get-tuple-element.234), channel_id=1, source_target_pairs={{0,8},{1,9},{2,10},{3,11},{4,12},{5,13},{6,14},{7,15},{8,16},{9,17... | collective-permute-start | bytes 294920
  2451.1 52.2 %collective-permute-start.70 = (f32[8,3072]{1,0:T(8,128)}, f32[8,3072]{1,0:T(8,128)S(1)}, u32[]{:S(2)}, u32[]{:S(2)}) collective-permute-start(f32[8,3072]{1,0:T(8,128)} %get-tuple-element.234), channel_id=1, source_target_pairs={{0,7},{1,8},{2,9},{3,10},{4,11},{5,12},{6,13},{7,14},{8,15},{9,16}... | collective-permute-start | bytes 294920
  2454.8 50.6 %collective-permute-start.69 = (f32[8,3072]{1,0:T(8,128)}, f32[8,3072]{1,0:T(8,128)}, u32[]{:S(2)}, u32[]{:S(2)}) collective-permute-start(f32[8,3072]{1,0:T(8,128)} %get-tuple-element.234), channel_id=1, source_target_pairs={{0,6},{1,7},{2,8},{3,9},{4,10},{5,11},{6,12},{7,13},{8,14},{9,15},... | collective-permute-start | bytes 294920
  (194 other events, 7421.6 us)
Sparse Core Ops, SparseCore 0:
  9.7 311.4 all-gather.10
  322.9 298.0 all-gather.12
  622.8 310.3 all-gather.14
  934.7 309.1 all-gather.8
  1255.5 652.8 reduce-scatter.8
where the time goes:
time: 2570 us; the launch traced here: 2550 us
  blocking collectives  1160 us (45%)
  waiting for transfers between devices  781 us (30%)
  starting transfers between devices  285 us (11%)
  local copies, waits for them, and re-layouts  185 us (7%)
  matrix products  105 us (4%)
    unnamed x3, blocking collectives  839 us
    all_gather x1, blocking collectives, per_device(): lax.all_gather(shards[6], ('grp', 'seq'), axis=1, tiled=True)  320 us
    all_gather x1, waiting for transfers between devices, per_device(): lax.all_gather(shards[3], ('grp', 'seq'), axis=0, tiled=True)  292 us
    unnamed x96, starting transfers between devices  269 us
    all_gather x1, waiting for transfers between devices, per_device(): lax.all_gather(shards[0], ('grp', 'seq'), axis=0, tiled=True)  238 us
    all_gather x1, waiting for transfers between devices, per_device(): lax.all_gather(shards[2], ('grp', 'seq'), axis=0, tiled=True)  219 us
    unnamed x262, local copies, waits for them, and re-layouts  130 us
  transfers between devices with their start and end apart: 105, of which 10 were waited for; matrix products, arithmetic and copies ran while one was open for 39% of the time, Pallas kernels for 0%

commit v1 on v0

v1 whole, which is shorter than its diff:
```python
import functools

import jax
import jax.numpy as jnp
from jax import lax
from jax.experimental import pallas as pl
from jax.experimental.pallas import tpu as pltpu
from jax.sharding import PartitionSpec as P

MESH = pl.DeviceIdType.MESH
F32 = jnp.float32
BF16 = jnp.bfloat16
EPS = 1e-05
D = 768
ROWS = 256
EXT = 512
PAIRS = 6
TILES = 18
BLOCK = (48, 384)
GRID = (2, 2, 2, 4, 2, 2)
VEC = 80
ORDERS = (("x", "y", "z"), ("y", "z", "x"), ("z", "x", "y"))
BACK = (("z", "y", "x"), ("x", "z", "y"), ("y", "x", "z"))
LIMIT = 60 * 2**20


class Place:
    def __init__(self, send_sem, recv_sem):
        grp, seq = lax.axis_index("grp"), lax.axis_index("seq")
        self.c = lax.rem(grp, 2)
        self.x = lax.rem(lax.div(grp, 2), 4)
        self.y = lax.rem(lax.div(grp, 8), 4)
        self.z = lax.div(grp, 32) * 2 + seq
        self.zl = seq
        self.index = grp * 2 + seq
        self.send_sem, self.recv_sem = send_sem, recv_sem
        self.used = 0
        self.sent = []

    def device(self, **new):
        at = {"x": self.x, "y": self.y, "z": self.z, "c": self.c}
        at.update(new)
        grp = ((lax.div(at["z"], 2) * 4 + at["y"]) * 4 + at["x"]) * 2 + at["c"]
        return (grp, lax.rem(at["z"], 2))

    def along(self, axis, delta):
        return lax.rem(getattr(self, axis) + delta, 4)

    def flip(self, value, bit):
        return value + bit * (1 - 2 * lax.rem(value, 2))

    def member(self, d):
        x, c, z = self.flip(self.x, d // 4), self.flip(self.c, (d // 2) % 2), self.flip(self.z, d % 2)
        number = lax.rem(x, 2) * 4 + c * 2 + lax.rem(z, 2)
        return self.device(x=x, c=c, z=z), number

    def greet(self):
        barrier = pltpu.get_barrier_semaphore()
        partners = [self.device(**{a: self.along(a, d)}) for a in "xyz" for d in (1, 2, 3)]
        partners += [self.member(d)[0] for d in (2, 3, 5, 6, 7)]
        for partner in partners:
            pl.semaphore_signal(barrier, inc=1, device_id=partner, device_id_type=MESH)
        pl.semaphore_wait(barrier, len(partners))

    def slot(self):
        self.used += 1
        return self.used - 1

    def copy(self, src, dst, device, slot):
        return pltpu.make_async_remote_copy(
            src_ref=src,
            dst_ref=dst,
            send_sem=self.send_sem.at[slot],
            recv_sem=self.recv_sem.at[slot],
            device_id=device,
            device_id_type=MESH,
        )

    def send(self, src, dst, device, slot):
        self.copy(src, dst, device, slot).start()
        self.sent.append((src, device, slot))

    def arrive(self, dst, slot):
        self.copy(dst, dst, self.device(), slot).wait_recv()

    def drain(self):
        for src, device, slot in self.sent:
            self.copy(src, src, device, slot).wait_send()
        self.sent = []


def slab(ref, lead=(), c=None, **at):
    index = list(lead) + [slice(None) if c is None else c]
    for axis in "zyx":
        value = at.get(axis)
        half = isinstance(value, tuple)
        if axis == "y":
            index.append(pl.ds(2 * value[1], 2) if half else slice(None) if value is None else value)
        elif half:
            index += [value[1], slice(None)]
        elif value is None:
            index += [slice(None), slice(None)]
        else:
            index += [lax.div(value, 2), lax.rem(value, 2)]
    return ref.at[tuple(index)]


def total_of(place, vec, incoming):
    for stage, axis in enumerate("cxyz"):
        steps = (1,) if axis == "c" else (1, 2, 3)
        slots = [place.slot() for _ in steps]
        for k, step in enumerate(steps):
            device = place.device(c=1 - place.c) if axis == "c" else place.device(**{axis: place.along(axis, step)})
            place.send(vec.at[stage], incoming.at[stage, k], device, slots[k])
        total = vec[stage]
        for k, step in enumerate(steps):
            place.arrive(incoming.at[stage, k], slots[k])
            total = total + incoming[stage, k]
        vec[stage + 1] = total
        yield


def spread(index, count, width):
    row = lax.broadcasted_iota(jnp.int32, (128, width), 0)
    column = lax.broadcasted_iota(jnp.int32, (128, width), 1)
    return jnp.where((column == count * index + row) & (row < count), 1.0, 0.0)


def gather_kernel(tok, wq, wo, wu, wd, ga, gf, taps, w_out, vec_out, prev, to_peer, from_peer, pile, down_s, down, few, vec, incoming, send_sem, recv_sem):
    place = Place(send_sem, recv_sem)
    c, zl = place.c, place.zl
    for number in range(8):
        source = wq[:, number * 384:(number + 1) * 384] if number < 6 else wo[:, (number - 6) * 384:(number - 5) * 384]
        to_peer[number, 0, 0:6, :] = source.astype(F32)
        to_peer[number, 1, 0:6, :] = wu[:, number * 384:(number + 1) * 384].astype(F32)
    left, right = wd[:, 0:384].astype(F32), wd[:, 384:768].astype(F32)
    down_s[...] = jnp.where(zl == 0, right, left)
    down[pl.ds(pl.multiple_of(zl * 24, 8), 24), :] = jnp.where(zl == 0, left, right)
    few[...] = jnp.zeros_like(few)
    few[0:1, 0:6] = ga[...].astype(F32)
    few[1:2, 0:6] = gf[...].astype(F32)
    few[2:5, 0:18] = taps[...].astype(F32)
    low = few[...].astype(BF16)
    gains = jnp.dot(low, spread(place.index, 6, D).astype(BF16), preferred_element_type=F32)
    tapped = jnp.dot(low, spread(place.index, 18, 3 * D).astype(BF16), preferred_element_type=F32)
    vec[0] = jnp.zeros((VEC, 128), F32)
    for r in range(6):
        vec[0, r:r + 1, :] = gains[0:1, r * 128:(r + 1) * 128]
        vec[0, 6 + r:7 + r, :] = gains[1:2, r * 128:(r + 1) * 128]
    for j in range(3):
        for t in range(TILES):
            row = 12 + TILES * j + t
            vec[0, row:row + 1, :] = tapped[2 + j:3 + j, t * 128:(t + 1) * 128]

    place.greet()
    other = place.device(z=place.flip(place.z, 1))
    trade = [place.slot() for _ in range(8)]
    _, mine = place.member(0)
    for d in range(1, 8):
        device, number = place.member(d)
        place.send(to_peer.at[number], from_peer.at[mine], device, trade[d])
    place.send(down_s, down.at[pl.ds(pl.multiple_of(zl * 24, 8), 24)], other, trade[0])
    token_slot = place.slot()

    @pl.when(zl == 0)
    def _():
        place.copy(tok, prev, other, token_slot).start()

    @pl.when(zl == 1)
    def _():
        place.arrive(prev, token_slot)

    @pl.when(zl == 0)
    def _():
        prev[...] = jnp.zeros_like(prev)

    sums = total_of(place, vec, incoming)
    from_peer[mine] = to_peer[mine]
    for d in range(1, 8):
        _, number = place.member(d)
        place.arrive(from_peer.at[number], trade[d])
    place.arrive(down.at[pl.ds(pl.multiple_of((1 - zl) * 24, 8), 24)], trade[0])
    for number in range(8):
        for k in range(2):
            pile[k, 6 * number:6 * number + 8, :] = from_peer[number, k]
    at = (c, lax.div(place.z, 2), zl, place.y, lax.div(place.x, 2), lax.rem(place.x, 2))
    for k in range(2):
        w_out[(k,) + at] = pile[k, 0:48, :].astype(BF16)
    w_out[(2,) + at] = down[...].astype(BF16)

    here = {"x": place.x, "y": place.y, "z": place.z}
    sibling = place.device(c=1 - c)
    passed = []

    def pass_on(part, spot):
        slot = place.slot()
        place.send(slab(w_out, (part,), c, **spot), slab(w_out, (part,), c, **spot), sibling, slot)
        passed.append((part, spot, slot))

    for stage in range(2):
        waits = []
        for part in range(3):
            axis, done = ORDERS[part][stage], ORDERS[part][:stage]
            spot = {a: here[a] for a in "xyz" if a not in done}
            for step in (1, 2, 3):
                slot = place.slot()
                piece = slab(w_out, (part,), c, **spot)
                place.send(piece, piece, place.device(**{axis: place.along(axis, step)}), slot)
                waits.append((part, {**spot, axis: place.along(axis, 4 - step)}, slot))
        next(sums)
        for part, spot, slot in waits:
            place.arrive(slab(w_out, (part,), c, **spot), slot)
    first = [[place.slot() for _ in range(4)] for _ in range(3)]
    for part in range(3):
        axis = ORDERS[part][2]
        piece = slab(w_out, (part,), c, **{axis: here[axis]})
        place.send(piece, piece, place.device(**{axis: place.along(axis, 1)}), first[part][0])
        place.send(piece, piece, place.device(**{axis: place.along(axis, 3)}), first[part][1])
        pass_on(part, {axis: here[axis]})
    next(sums)
    for side in range(2):
        for part in range(3):
            axis, whole = ORDERS[part][2], ORDERS[part][0]
            came = {axis: place.along(axis, 3 if side == 0 else 1)}
            place.arrive(slab(w_out, (part,), c, **came), first[part][side])
            piece = slab(w_out, (part,), c, **came, **{whole: ("half", side)})
            place.send(piece, piece, place.device(**{axis: place.along(axis, 1 if side == 0 else 3)}), first[part][2 + side])
            pass_on(part, came)
    next(sums)
    for side in range(2):
        for part in range(3):
            axis, whole = ORDERS[part][2], ORDERS[part][0]
            came = {axis: place.along(axis, 2), whole: ("half", side)}
            place.arrive(slab(w_out, (part,), c, **came), first[part][2 + side])
            pass_on(part, came)
    vec_out[...] = vec[4]
    for part, spot, slot in passed:
        place.arrive(slab(w_out, (part,), 1 - c, **spot), slot)
    place.drain()

    @pl.when(zl == 0)
    def _():
        place.copy(tok, tok, other, token_slot).wait_send()


def gather(tok, wq, wo, wu, wd, ga, gf, taps):
    vmem = pl.BlockSpec(memory_space=pltpu.VMEM)
    return pl.pallas_call(
        gather_kernel,
        out_shape=(
            jax.ShapeDtypeStruct((3,) + GRID + BLOCK, BF16),
            jax.ShapeDtypeStruct((VEC, 128), F32),
            jax.ShapeDtypeStruct((ROWS, D), BF16),
        ),
        in_specs=[vmem] * 8,
        out_specs=(vmem,) * 3,
        scratch_shapes=[
            pltpu.VMEM((8, 2, 8, 384), F32),
            pltpu.VMEM((8, 2, 8, 384), F32),
            pltpu.VMEM((2, 56, 384), F32),
            pltpu.VMEM((24, 384), F32),
            pltpu.VMEM((48, 384), F32),
            pltpu.VMEM((8, 128), F32),
            pltpu.VMEM((5, VEC, 128), F32),
            pltpu.VMEM((4, 3, VEC, 128), F32),
            pltpu.SemaphoreType.DMA((80,)),
            pltpu.SemaphoreType.DMA((80,)),
        ],
        compiler_params=pltpu.CompilerParams(collective_id=0, has_side_effects=True, vmem_limit_bytes=LIMIT),
    )(tok, wq, wo, wu, wd, ga, gf, taps)


def nt(left, right):
    return lax.dot_general(left, right, (((1,), (1,)), ((), ())), preferred_element_type=F32)


def tn(left, right):
    return lax.dot_general(left, right, (((0,), (0,)), ((), ())), preferred_element_type=F32)


def nn(left, right):
    return jnp.dot(left, right, preferred_element_type=F32)


def columns(ref, part, jp):
    halves = [ref[part, lax.rem(jp, 2), :, zl, :, :, lax.div(jp, 2)].reshape(D, 384) for zl in range(2)]
    return jnp.concatenate(halves, axis=1)


def put_columns(ref, part, jp, value):
    for zl in range(2):
        ref[part, lax.rem(jp, 2), :, zl, :, :, lax.div(jp, 2)] = (
            value[:, zl * 384:(zl + 1) * 384].astype(BF16).reshape(2, 4, 2, 48, 384)
        )


def row_pieces():
    return [(y, xh, xl, c) for y in range(2) for xh in range(2) for xl in range(2) for c in range(2)]


def rows(ref, jp):
    zh, y0 = lax.div(jp, 2), lax.rem(jp, 2) * 2
    halves = [
        jnp.concatenate([ref[2, c, zh, zl, y0 + y, xh, xl] for y, xh, xl, c in row_pieces()], axis=0) for zl in range(2)
    ]
    return jnp.concatenate(halves, axis=1)


def put_rows(ref, jp, value):
    zh, y0 = lax.div(jp, 2), lax.rem(jp, 2) * 2
    low = value.astype(BF16)
    for zl in range(2):
        for k, (y, xh, xl, c) in enumerate(row_pieces()):
            ref[2, c, zh, zl, y0 + y, xh, xl] = low[48 * k:48 * k + 48, zl * 384:(zl + 1) * 384]


def normalize(values):
    mean = jnp.mean(values, axis=-1, keepdims=True)
    centred = values - mean
    inverse = lax.rsqrt(jnp.mean(centred * centred, axis=-1, keepdims=True) + EPS)
    return centred * inverse, inverse


def norm_back(grad, normed, inverse):
    first = jnp.mean(grad, axis=-1, keepdims=True)
    second = jnp.mean(grad * normed, axis=-1, keepdims=True)
    return inverse * (grad - first - normed * second)


def shifted(values, steps):
    count = values.shape[0]
    row = lax.broadcasted_iota(jnp.int32, values.shape, 0)
    rolled = pltpu.roll(values, steps % count, 0)
    return jnp.where(row >= steps if steps > 0 else row < count + steps, rolled, 0.0)


def layer_kernel(tok, prev, cot, w, vec, out, partial, contrib, g, gvec, h1, n1, inv1, raw, mixed, bias, probs, att, h2, gh2, gatt, gqkv, gh1, acc):
    rank = lax.axis_index("seq")
    gain_one = jnp.concatenate([vec[r:r + 1, :] for r in range(6)], axis=1)
    gain_two = jnp.concatenate([vec[r:r + 1, :] for r in range(6, 12)], axis=1)
    gvec[...] = jnp.zeros_like(gvec)
    for half in range(2):
        values = (prev if half == 0 else tok)[...].astype(F32)
        normed, inverse = normalize(values)
        here = pl.ds(half * ROWS, ROWS)
        n1[here, :] = normed
        inv1[here, :] = inverse
        h1[here, :] = (normed * gain_one).astype(BF16)

    def tap(j, t):
        return vec[pl.ds(12 + TILES * j + t, 1), :]

    @pl.loop(0, 3)
    def _(jp):
        block = nn(h1[...], columns(w, 0, jp)).astype(BF16)
        for k in range(6):
            t = 6 * jp + k
            tile = block[:, 128 * k:128 * (k + 1)]
            raw[t] = tile
            value = tile.astype(F32)
            conv = tap(0, t) * value + tap(1, t) * shifted(value, 1) + tap(2, t) * shifted(value, 2)
            mixed[t] = conv.astype(BF16)

    row = lax.broadcasted_iota(jnp.int32, (ROWS, EXT), 0)
    column = lax.broadcasted_iota(jnp.int32, (ROWS, EXT), 1)
    behind = jnp.where(column < ROWS, (1 - rank) * EXT, column - ROWS)
    bias[...] = jnp.where(behind <= row, 0.0, -1e30)
    first = lax.broadcasted_iota(jnp.int32, (ROWS, 128), 1) < 64

    def both(value):
        zero = jnp.zeros_like(value)
        return jnp.concatenate([jnp.where(first, value, zero), jnp.where(first, zero, value)], axis=0)

    def pick(value):
        return jnp.where(first, value[:ROWS], value[ROWS:])

    @pl.loop(0, PAIRS)
    def _(p):
        query = both(mixed[p, ROWS:, :])
        key, value = mixed[PAIRS + p], mixed[2 * PAIRS + p]
        scores = nt(query, key) * 0.125 + jnp.concatenate([bias[...], bias[...]], axis=0)
        weights = jnp.exp(scores - jnp.max(scores, axis=-1, keepdims=True))
        exact = weights * (1.0 / jnp.sum(weights, axis=-1, keepdims=True))
        probs[p] = exact
        att[p] = pick(nn(exact.astype(BF16), value)).astype(BF16)

    attended = jnp.concatenate([att[p] for p in range(PAIRS)], axis=1)
    resid = tok[...].astype(F32) + nn(attended, columns(w, 0, 3))
    normed_two, inverse_two = normalize(resid)
    h2[...] = (normed_two * gain_two).astype(BF16)
    acc[...] = resid
    gh2[...] = jnp.zeros_like(gh2)

    @pl.loop(0, 4)
    def _(jp):
        up = columns(w, 1, jp)
        down = rows(w, jp)
        rect = jnp.maximum(nn(h2[...], up), 0.0)
        act = (rect * rect).astype(BF16)
        acc[...] += nn(act, down)
        gact = nt(cot[...], down)
        put_rows(g, jp, tn(act, cot[...]))
        gup = (gact * 2.0 * rect).astype(BF16)
        put_columns(g, 1, jp, tn(h2[...], gup))
        gh2[...] += nt(gup, up)

    out[...] = acc[...].astype(BF16)
    grad_two = gh2[...]
    summed = jnp.sum(grad_two * normed_two, axis=0, keepdims=True)
    for r in range(6):
        gvec[6 + r:7 + r, :] = summed[:, 128 * r:128 * (r + 1)]
    grad_resid = cot[...].astype(F32) + norm_back(grad_two * gain_two, normed_two, inverse_two)
    acc[...] = grad_resid
    gproj = grad_resid.astype(BF16)
    put_columns(g, 0, 3, tn(attended, gproj))
    gback = nt(gproj, columns(w, 0, 3)).astype(BF16)
    for p in range(PAIRS):
        gatt[p] = gback[:, 128 * p:128 * (p + 1)]

    @pl.loop(0, PAIRS)
    def _(p):
        query = both(mixed[p, ROWS:, :])
        key, value = mixed[PAIRS + p], mixed[2 * PAIRS + p]
        grad = both(gatt[p])
        exact = probs[p]
        gvalue = tn(exact.astype(BF16), grad)
        gprobs = nt(grad, value)
        centred = gprobs - jnp.sum(gprobs * exact, axis=-1, keepdims=True)
        gscores = (exact * centred).astype(BF16)
        gquery = pick(nn(gscores, key)) * 0.125
        gkey = tn(gscores, query) * 0.125
        for k, tile in enumerate((jnp.concatenate([jnp.zeros_like(gquery), gquery], axis=0), gkey, gvalue)):
            t = PAIRS * k + p
            back = tap(0, t) * tile + tap(1, t) * shifted(tile, -1) + tap(2, t) * shifted(tile, -2)
            gqkv[t] = back.astype(BF16)
            value_in = raw[t].astype(F32)
            for j in range(3):
                delayed = value_in if j == 0 else shifted(value_in, j)
                gvec[pl.ds(12 + TILES * j + t, 1), :] = jnp.sum(tile * delayed, axis=0, keepdims=True)

    gh1[...] = jnp.zeros_like(gh1)

    @pl.loop(0, 3)
    def _(jp):
        grad = jnp.concatenate([gqkv[6 * jp + k] for k in range(6)], axis=1)
        put_columns(g, 0, jp, tn(h1[...], grad))
        gh1[...] += nt(grad, columns(w, 0, jp))

    total = jnp.zeros((1, D), F32)
    for half in range(2):
        here = pl.ds(half * ROWS, ROWS)
        grad_one = gh1[here, :]
        total = total + jnp.sum(grad_one * n1[here, :], axis=0, keepdims=True)
        back = norm_back(grad_one * gain_one, n1[here, :], inv1[here, :])
        if half == 0:
            contrib[...] = back.astype(BF16)
        else:
            partial[...] = acc[...] + back
    for r in range(6):
        gvec[r:r + 1, :] = total[:, 128 * r:128 * (r + 1)]


def layer(tok, prev, cot, w, vec):
    vmem = pl.BlockSpec(memory_space=pltpu.VMEM)
    return pl.pallas_call(
        layer_kernel,
        out_shape=(
            jax.ShapeDtypeStruct((ROWS, D), BF16),
            jax.ShapeDtypeStruct((ROWS, D), F32),
            jax.ShapeDtypeStruct((ROWS, D), BF16),
            jax.ShapeDtypeStruct((3,) + GRID + BLOCK, BF16),
            jax.ShapeDtypeStruct((VEC, 128), F32),
        ),
        in_specs=[vmem] * 5,
        out_specs=(vmem,) * 5,
        scratch_shapes=[
            pltpu.VMEM((EXT, D), BF16),
            pltpu.VMEM((EXT, D), F32),
            pltpu.VMEM((EXT, 1), F32),
            pltpu.VMEM((TILES, EXT, 128), BF16),
            pltpu.VMEM((TILES, EXT, 128), BF16),
            pltpu.VMEM((ROWS, EXT), F32),
            pltpu.VMEM((PAIRS, EXT, EXT), F32),
            pltpu.VMEM((PAIRS, ROWS, 128), BF16),
            pltpu.VMEM((ROWS, D), BF16),
            pltpu.VMEM((ROWS, D), F32),
            pltpu.VMEM((PAIRS, ROWS, 128), BF16),
            pltpu.VMEM((TILES, EXT, 128), BF16),
            pltpu.VMEM((EXT, D), F32),
            pltpu.VMEM((ROWS, D), F32),
        ],
        compiler_params=pltpu.CompilerParams(vmem_limit_bytes=LIMIT),
    )(tok, prev, cot, w, vec)


def kept(axes):
    grid = []
    for axis in "zyx":
        if axis not in axes:
            grid += {"z": [2, 2], "y": [4], "x": [2, 2]}[axis]
    return tuple(grid)


def flat(grid):
    count = 1
    for n in grid:
        count *= n
    return count


def unflat(k, grid):
    index = []
    for n in reversed(grid):
        index.insert(0, lax.rem(k, n))
        k = lax.div(k, n)
    return index


def reduce_kernel(partial, contrib, gvec, g_in, gtok, gq, go, gu, gd, gga, ggf, gtap, g, from_core, *scratch):
    lands, (got, vec, incoming, pieces, arrived, down, sums, load_sem, send_sem, recv_sem) = scratch[:9], scratch[9:]
    load = pltpu.make_async_copy(g_in, g, load_sem)
    load.start()
    place = Place(send_sem, recv_sem)
    c, zl = place.c, place.zl
    place.greet()
    load.wait()
    here = {"x": place.x, "y": place.y, "z": place.z}
    sibling = place.device(c=1 - c)
    other = place.device(z=place.flip(place.z, 1))
    token_slot = place.slot()

    @pl.when(zl == 1)
    def _():
        place.copy(contrib, got, other, token_slot).start()

    core = [place.slot() for _ in range(3)]
    for part in range(3):
        place.send(slab(g, (part,), 1 - c), from_core.at[part], sibling, core[part])
    vec[0] = gvec[...]
    small = total_of(place, vec, incoming)
    next(small)
    for part in range(3):
        place.arrive(from_core.at[part], core[part])

        @pl.loop(0, 64)
        def _(k):
            at = unflat(k, (2, 2, 4, 2, 2))
            spot = (part, c, *at)
            g[spot] = (g[spot].astype(F32) + from_core[(part, *at)].astype(F32)).astype(BF16)

    stages = [lands[3 * stage:3 * stage + 3] for stage in range(3)]
    for stage in range(3):
        waits = []
        for part in range(3):
            axis, done = BACK[part][stage], BACK[part][:stage]
            spot = {a: here[a] for a in done}
            for step in (1, 2, 3):
                slot = place.slot()
                there = place.along(axis, step)
                place.send(slab(g, (part,), c, **{**spot, axis: there}), stages[stage][part].at[step - 1], place.device(**{axis: there}), slot)
                waits.append(slot)
        next(small)
        for part in range(3):
            axis, done = BACK[part][stage], BACK[part][:stage]
            for step in (1, 2, 3):
                place.arrive(stages[stage][part].at[step - 1], waits[part * 3 + step - 1])
            spot = {a: here[a] for a in done + (axis,)}
            grid = kept(done + (axis,))
            land = stages[stage][part]

            def add(at):
                index, rest = [part, c], list(at)
                for a in "zyx":
                    if a in spot:
                        index += [spot[a]] if a == "y" else [lax.div(spot[a], 2), lax.rem(spot[a], 2)]
                    elif a == "y":
                        index.append(rest.pop(0))
                    else:
                        index += [rest.pop(0), rest.pop(0)]
                index = tuple(index)
                total = g[index].astype(F32)
                for step in range(3):
                    total = total + land[(step, *at)].astype(F32)
                if stage < 2:
                    g[index] = total.astype(BF16)
                else:
                    sums[part] = total

            if stage == 2:
                add(())
            else:
                pl.loop(0, flat(grid))(lambda k: add(unflat(k, grid)))
    _, mine = place.member(0)
    for number in range(8):
        for k in range(2):
            pieces[number, k, 0:6, :] = sums[k, 6 * number:6 * number + 6, :]
            pieces[number, k, 6:8, :] = jnp.zeros((2, 384), F32)
    trade = [place.slot() for _ in range(8)]
    for d in range(1, 8):
        device, number = place.member(d)
        place.send(pieces.at[number], arrived.at[mine], device, trade[d])
    place.send(sums.at[2, pl.ds(pl.multiple_of((1 - zl) * 24, 8), 24)], down, other, trade[0])
    arrived[mine] = pieces[mine]
    summed = vec[4]
    gains = [jnp.concatenate([summed[r:r + 1] for r in range(6 * k, 6 * k + 6)], axis=1) for k in range(2)]
    tapped = [jnp.concatenate([summed[r:r + 1] for r in range(12 + TILES * j, 12 + TILES * j + TILES)], axis=1) for j in range(3)]
    gain_rows = jnp.concatenate(gains + [jnp.zeros((6, D), F32)], axis=0)
    tap_rows = jnp.concatenate(tapped + [jnp.zeros((5, 3 * D), F32)], axis=0)
    high = functools.partial(
        lax.dot_general,
        dimension_numbers=(((1,), (1,)), ((), ())),
        preferred_element_type=F32,
        precision=lax.Precision.HIGHEST,
    )
    gain_own = high(gain_rows, spread(place.index, 6, D))
    gga[...] = gain_own[0:1, 0:6]
    ggf[...] = gain_own[1:2, 0:6]
    gtap[...] = high(tap_rows, spread(place.index, 18, 3 * D))[0:3, 0:18]

    @pl.when(zl == 0)
    def _():
        place.arrive(got, token_slot)

    @pl.when(zl == 1)
    def _():
        got[...] = jnp.zeros_like(got)

    gtok[...] = (partial[...] + got[...].astype(F32)).astype(BF16)
    for d in range(1, 8):
        _, number = place.member(d)
        place.arrive(arrived.at[number], trade[d])
    place.arrive(down, trade[0])
    for number in range(8):
        if number < 6:
            gq[:, 384 * number:384 * (number + 1)] = arrived[number, 0, 0:6, :]
        else:
            go[:, 384 * (number - 6):384 * (number - 5)] = arrived[number, 0, 0:6, :]
        gu[:, 384 * number:384 * (number + 1)] = arrived[number, 1, 0:6, :]
    own = sums[2, pl.ds(pl.multiple_of(zl * 24, 8), 24), :]
    gd[:, 0:384] = jnp.where(zl == 0, own, down[...])
    gd[:, 384:768] = jnp.where(zl == 0, down[...], own)
    place.drain()

    @pl.when(zl == 1)
    def _():
        place.copy(contrib, contrib, other, token_slot).wait_send()


def reduce(partial, contrib, gvec, g):
    vmem = pl.BlockSpec(memory_space=pltpu.VMEM)
    lands = []
    for stage in range(3):
        for part in range(3):
            grid = kept(BACK[part][:stage + 1])
            lands.append(pltpu.VMEM((3,) + grid + BLOCK, BF16))
    return pl.pallas_call(
        reduce_kernel,
        out_shape=(
            jax.ShapeDtypeStruct((ROWS, D), BF16),
            jax.ShapeDtypeStruct((6, 2304), F32),
            jax.ShapeDtypeStruct((6, 768), F32),
            jax.ShapeDtypeStruct((6, 3072), F32),
            jax.ShapeDtypeStruct((24, 768), F32),
            jax.ShapeDtypeStruct((1, 6), F32),
            jax.ShapeDtypeStruct((1, 6), F32),
            jax.ShapeDtypeStruct((3, 18), F32),
        ),
        in_specs=[vmem] * 3 + [pl.BlockSpec(memory_space=pl.ANY)],
        out_specs=(vmem,) * 8,
        scratch_shapes=[
            pltpu.VMEM((3,) + GRID + BLOCK, BF16),
            pltpu.VMEM((3,) + GRID[1:] + BLOCK, BF16),
            *lands,
            pltpu.VMEM((ROWS, D), BF16),
            pltpu.VMEM((5, VEC, 128), F32),
            pltpu.VMEM((4, 3, VEC, 128), F32),
            pltpu.VMEM((8, 2, 8, 384), F32),
            pltpu.VMEM((8, 2, 8, 384), F32),
            pltpu.VMEM((24, 384), F32),
            pltpu.VMEM((3,) + BLOCK, F32),
            pltpu.SemaphoreType.DMA,
            pltpu.SemaphoreType.DMA((64,)),
            pltpu.SemaphoreType.DMA((64,)),
        ],
        compiler_params=pltpu.CompilerParams(collective_id=1, has_side_effects=True, vmem_limit_bytes=LIMIT),
    )(partial, contrib, gvec, g)


def per_device(tokens, w_qkv, w_out, w_up, w_down, gain_attn, gain_ffn, conv_taps, cotangent):
    w, vec, prev = gather(
        tokens, w_qkv, w_out, w_up, w_down, gain_attn.reshape(1, 6), gain_ffn.reshape(1, 6), conv_taps
    )
    out, partial, contrib, g, gvec = layer(tokens, prev, cotangent, w, vec)
    gtok, gq, go, gu, gd, gga, ggf, gtap = reduce(partial, contrib, gvec, g)
    return out, gtok, gq, go, gu, gd, gga.reshape(6), ggf.reshape(6), gtap


def solution(mesh):
    both = ("grp", "seq")
    row, one, column = P(both, None), P(both), P(None, both)
    return jax.shard_map(
        per_device,
        mesh=mesh,
        in_specs=(row, row, row, row, row, one, one, column, row),
        out_specs=(row, row, row, row, row, row, one, one, column),
        check_vma=False,
    )
```

time: 2570 us -> 198 us (0.08)
  blocking collectives: 1160 us -> 0 us
  waiting for transfers between devices: 781 us -> 0 us
  starting transfers between devices: 285 us -> 0 us
  Pallas kernels: 0 us -> 186 us
  local copies, waits for them, and re-layouts: 185 us -> 11.3 us
  matrix products: 105 us -> 0 us
    unnamed x3 -> x0, blocking collectives: 839 us -> none
    all_gather x4 -> x0, waiting for transfers between devices: 750 us -> none  [the longest x1 292 us: per_device(): lax.all_gather(shards[3], ('grp', 'seq'), axis=0, tiled=True)]
    all_gather x1 -> x0, blocking collectives: 320 us -> none  [per_device(): lax.all_gather(shards[6], ('grp', 'seq'), axis=1, tiled=True)]
    unnamed x96 -> x0, starting transfers between devices: 269 us -> none
    pallas_call x0 -> x3, Pallas kernels: none -> 186 us  [the longest x1 74.7 us: reduce(): pl.pallas_call(reduce_kernel, out_shape=(jax.ShapeDtypeStruct((ROWS, D),...]
    unnamed x262 -> x8, local copies, waits for them, and re-layouts: 130 us -> 11.3 us
    dot_general x54 -> x0, matrix products: 105 us -> none  [the longest x4 17.3 us: contract_rows(): lax.dot_general(left, right, (((0,), (0,)), ((), ())), preferred_element_...]
  transfers between devices with their start and end apart: 105 -> 0, of which waited for: 10 -> 0; matrix products, arithmetic and copies ran while one was open for 39% -> 0% of each run, Pallas kernels for 0% -> 0%
where the time goes in v1:
time: 198 us
  Pallas kernels  186 us (94%)
  local copies, waits for them, and re-layouts  11.3 us (6%)
    pallas_call x1, Pallas kernels, reduce(): pl.pallas_call(reduce_kernel, out_shape=(jax.ShapeDtypeStruct((ROWS, D),...  74.7 us
    pallas_call x1, Pallas kernels, gather(): pl.pallas_call(gather_kernel, out_shape=(jax.ShapeDtypeStruct((3,) + GRID...  69.1 us
    pallas_call x1, Pallas kernels, layer(): pl.pallas_call(layer_kernel, out_shape=(jax.ShapeDtypeStruct((ROWS, D), B...  42 us
    unnamed x8, local copies, waits for them, and re-layouts  11.3 us

profile of v1, /device:TPU:1, one launch (start us, length us, event | category | flops | bytes accessed | tf_op | source)
XLA Modules:
  0.0 197.8 jit_solution(8872897166199224671)
XLA Ops:
  0.6 69.1 %shard_map.160 = (bf16[3,2,2,2,4,2,2,48,384]{8,7,6,5,4,3,2,1,0:T(8,128)(2,1)}, f32[80,128]{1,0:T(8,128)}, bf16[256,768]{1,0:T(8,128)(2,1)}) custom-call(bf16[256,768]{1,0:T(8,128)(2,1)} %tok.3, bf16[6,2304]{1,0:T(8,128)(2,1)} %wq.1, bf16[6,768]{1,0:T(8,128)(2,1)} %wo.1, bf16[6,3072]{1,0:T(8,128)(2,1)} %wu.1, bf16[24,768]{1,0:T(8,128)(2,1)} %wd.1, ...), custom_call_target="tpu_custom_call" | custom-call | tf_op jit(solution)/shard_map/pallas_call | solution.py:248
  69.8 42.0 %shard_map.161 = (bf16[256,768]{1,0:T(8,128)(2,1)}, f32[256,768]{1,0:T(8,128)}, bf16[256,768]{1,0:T(8,128)(2,1)}, bf16[3,2,2,2,4,2,2,48,384]{8,7,6,5,4,3,2,1,0:T(8,128)(2,1)}, f32[80,128]{1,0:T(8,128)}) custom-call(bf16[256,768]{1,0:T(8,128)(2,1)} %tok.3, bf16[256,768]{1,0:T(8,128)(2,1)} %get-tuple-element.25.prev, bf16[256,768]{1,0:T(8,128)(2,1)} %cot.1, ...), custom_call_target="tpu_custom_call" | custom-call | tf_op jit(solution)/shard_map/pallas_call | solution.py:465
  111.8 74.7 %shard_map.162 = (bf16[256,768]{1,0:T(8,128)(2,1)}, f32[6,2304]{1,0:T(8,128)}, f32[6,768]{1,0:T(8,128)}, f32[6,3072]{1,0:T(8,128)}, f32[24,768]{1,0:T(8,128)}, /...) custom-call(f32[256,768]{1,0:T(8,128)} %get-tuple-element.29.partial, bf16[256,768]{1,0:T(8,128)(2,1)} %get-tuple-element.30.contrib, ...), custom_call_target="tpu_custom_call" | custom-call | tf_op jit(solution)/shard_map/pallas_call | solution.py:656
  186.4 1.8 copy.26
  188.2 1.5 copy.27
  189.7 1.3 copy.28
  191.1 1.5 copy.29
  192.6 1.5 copy.30
  194.1 1.2 copy.31
  195.3 1.2 copy.32
  196.5 1.3 copy.33

commit v2 on v1

v2 whole, which is shorter than its diff:
```python
import functools

import jax
import jax.numpy as jnp
from jax import lax
from jax.experimental import pallas as pl
from jax.experimental.pallas import tpu as pltpu
from jax.sharding import PartitionSpec as P

MESH = pl.DeviceIdType.MESH
F32 = jnp.float32
BF16 = jnp.bfloat16
EPS = 1e-05
D = 768
ROWS = 256
EXT = 512
PAIRS = 6
TILES = 18
BLOCK = (48, 384)
GRID = (2, 2, 2, 4, 2, 2)
VEC = 80
ORDERS = (("x", "y", "z"), ("y", "z", "x"), ("z", "x", "y"))
BACK = (("z", "y", "x"), ("x", "z", "y"), ("y", "x", "z"))
LIMIT = 60 * 2**20


class Place:
    def __init__(self, send_sem, recv_sem):
        grp, seq = lax.axis_index("grp"), lax.axis_index("seq")
        self.c = lax.rem(grp, 2)
        self.x = lax.rem(lax.div(grp, 2), 4)
        self.y = lax.rem(lax.div(grp, 8), 4)
        self.z = lax.div(grp, 32) * 2 + seq
        self.zl = seq
        self.index = grp * 2 + seq
        self.send_sem, self.recv_sem = send_sem, recv_sem
        self.used = 0
        self.sent = []

    def device(self, **new):
        at = {"x": self.x, "y": self.y, "z": self.z, "c": self.c}
        at.update(new)
        grp = ((lax.div(at["z"], 2) * 4 + at["y"]) * 4 + at["x"]) * 2 + at["c"]
        return (grp, lax.rem(at["z"], 2))

    def along(self, axis, delta):
        return lax.rem(getattr(self, axis) + delta, 4)

    def flip(self, value, bit):
        return value + bit * (1 - 2 * lax.rem(value, 2))

    def member(self, d):
        x, c, z = self.flip(self.x, d // 4), self.flip(self.c, (d // 2) % 2), self.flip(self.z, d % 2)
        number = lax.rem(x, 2) * 4 + c * 2 + lax.rem(z, 2)
        return self.device(x=x, c=c, z=z), number

    def greet(self):
        barrier = pltpu.get_barrier_semaphore()
        partners = [self.device(**{a: self.along(a, d)}) for a in "xyz" for d in (1, 2, 3)]
        partners += [self.member(d)[0] for d in (2, 3, 5, 7)]
        partners += [self.device(x=self.along("x", d), c=1 - self.c) for d in (1, 2, 3)]
        for partner in partners:
            pl.semaphore_signal(barrier, inc=1, device_id=partner, device_id_type=MESH)
        return lambda: pl.semaphore_wait(barrier, len(partners))

    def slot(self):
        self.used += 1
        return self.used - 1

    def copy(self, src, dst, device, slot):
        return pltpu.make_async_remote_copy(
            src_ref=src,
            dst_ref=dst,
            send_sem=self.send_sem.at[slot],
            recv_sem=self.recv_sem.at[slot],
            device_id=device,
            device_id_type=MESH,
        )

    def send(self, src, dst, device, slot):
        self.copy(src, dst, device, slot).start()
        self.sent.append((src, device, slot))

    def arrive(self, dst, slot):
        self.copy(dst, dst, self.device(), slot).wait_recv()

    def drain(self):
        for src, device, slot in self.sent:
            self.copy(src, src, device, slot).wait_send()
        self.sent = []


def spot(lead, c=None, tail=(), **at):
    index = list(lead) + [slice(None) if c is None else c]
    for axis in "zyx":
        value = at.get(axis)
        half = isinstance(value, tuple)
        if axis == "y":
            index.append(pl.ds(2 * value[1], 2) if half else slice(None) if value is None else value)
        elif half:
            index += [value[1], slice(None)]
        elif value is None:
            index += [slice(None), slice(None)]
        else:
            index += [lax.div(value, 2), lax.rem(value, 2)]
    return tuple(index) + tail


def strip(sub):
    return (pl.ds(16 * sub, 16), slice(None))


def spread(index, count, width):
    row = lax.broadcasted_iota(jnp.int32, (128, width), 0)
    column = lax.broadcasted_iota(jnp.int32, (128, width), 1)
    return jnp.where((column == count * index + row) & (row < count), 1.0, 0.0)


def gather_strip(place, w, part, sub):
    order, c, tail = ORDERS[sub], place.c, strip(sub)
    here = {"x": place.x, "y": place.y, "z": place.z}
    sibling = place.device(c=1 - c)
    passed = []

    def piece(core, **at):
        return w.at[spot((part,), core, tail, **at)]

    def pass_on(**at):
        slot = place.slot()
        place.send(piece(c, **at), piece(c, **at), sibling, slot)
        passed.append((at, slot))

    for stage in range(2):
        axis, done = order[stage], order[:stage]
        own = {a: here[a] for a in "xyz" if a not in done}
        waits = []
        for step in (1, 2, 3):
            slot = place.slot()
            place.send(piece(c, **own), piece(c, **own), place.device(**{axis: place.along(axis, step)}), slot)
            waits.append(({**own, axis: place.along(axis, 4 - step)}, slot))
        yield
        for at, slot in waits:
            place.arrive(piece(c, **at), slot)
    axis, whole = order[2], order[0]
    slots = [place.slot() for _ in range(4)]
    toward = [place.device(**{axis: place.along(axis, 1)}), place.device(**{axis: place.along(axis, 3)})]
    for side in range(2):
        own = piece(c, **{axis: here[axis]})
        place.send(own, own, toward[side], slots[side])
    pass_on(**{axis: here[axis]})
    yield
    for side in range(2):
        came = {axis: place.along(axis, 3 if side == 0 else 1)}
        place.arrive(piece(c, **came), slots[side])
        half = piece(c, **came, **{whole: ("half", side)})
        place.send(half, half, toward[side], slots[2 + side])
        pass_on(**came)
    yield
    for side in range(2):
        came = {axis: place.along(axis, 2), whole: ("half", side)}
        place.arrive(piece(c, **came), slots[2 + side])
        pass_on(**came)
    yield
    for at, slot in passed:
        place.arrive(piece(1 - c, **at), slot)


HALF = {"z": "y", "x": "z", "y": "x"}
HALVES = {"z": (2, 2, 2), "x": (2, 4), "y": (2, 2, 2)}


def half_of(axis, h):
    return {"z": (pl.ds(2 * h, 2),), "x": (h,), "y": (slice(None), slice(None), h)}[axis]


def scatter_strip(place, w, part, sub, from_core, lands, sums):
    order, c, tail = BACK[sub], place.c, strip(sub)
    here = {"x": place.x, "y": place.y, "z": place.z}
    relay, low, high, second, third = lands

    def at(**where):
        return spot((part,), c, tail, **where)

    slot = place.slot()
    landed = (part,) + (slice(None),) * 5 + tail
    place.send(w.at[spot((part,), 1 - c, tail)], from_core.at[landed], place.device(c=1 - c), slot)
    yield
    place.arrive(from_core.at[landed], slot)
    w[at()] = w[at()] + from_core[landed]
    axis = order[0]
    up, down, across = place.along(axis, 1), place.along(axis, 3), place.along(axis, 2)
    whole = HALF[axis]
    above, below = place.device(**{axis: up}), place.device(**{axis: down})
    slots = [place.slot() for _ in range(6)]
    place.send(w.at[at(**{axis: across, whole: ("half", 0)})], relay.at[0], above, slots[0])
    place.send(w.at[at(**{axis: across, whole: ("half", 1)})], relay.at[1], below, slots[1])
    place.send(w.at[at(**{axis: up, whole: ("half", 1)})], low.at[half_of(axis, 1)], above, slots[2])
    place.send(w.at[at(**{axis: down, whole: ("half", 0)})], high.at[half_of(axis, 0)], below, slots[3])
    yield
    for side, (coordinate, device, land) in enumerate(((up, above, low), (down, below, high))):
        place.arrive(relay.at[side], slots[side])
        index = at(**{axis: coordinate, whole: ("half", side)})
        w[index] = w[index] + relay[side]
        place.send(w.at[index], land.at[half_of(axis, side)], device, slots[4 + side])
    yield
    place.arrive(low.at[half_of(axis, 1)], slots[2])
    place.arrive(high.at[half_of(axis, 0)], slots[3])
    place.arrive(low.at[half_of(axis, 0)], slots[4])
    place.arrive(high.at[half_of(axis, 1)], slots[5])
    index = at(**{axis: here[axis]})
    w[index] = (w[index].astype(F32) + low[...].astype(F32) + high[...].astype(F32)).astype(BF16)
    for stage, land in ((1, second), (2, third)):
        axis, done = order[stage], order[:stage]
        own = {a: here[a] for a in done}
        slots = [place.slot() for _ in range(3)]
        for step in (1, 2, 3):
            there = place.along(axis, step)
            place.send(w.at[at(**own, **{axis: there})], land.at[step - 1], place.device(**{axis: there}), slots[step - 1])
        yield
        for step in range(3):
            place.arrive(land.at[step], slots[step])
        index = at(**own, **{axis: here[axis]})
        total = w[index].astype(F32)
        for step in range(3):
            total = total + land[step].astype(F32)
        if stage == 1:
            w[index] = total.astype(BF16)
        else:
            sums[part, 16 * sub:16 * sub + 16, :] = total


def advance(steps):
    for step in steps:
        next(step, None)


def remainder(value, count):
    value = value.astype(F32)
    whole = jnp.floor((value + 0.5) * (1.0 / count))
    return value - whole * count, whole


def gather_vectors(place, few, tiles, landed, vec):
    slots = [place.slot() for _ in range(7)]
    sublane = lax.broadcasted_iota(jnp.int32, (8, 128), 0)
    mine = place.c * 4 + place.x
    own = jnp.where(sublane == mine, few[...], 0.0)
    here = tiles.at[place.z, place.y]
    landed[7] = own
    yield
    for k in range(7):
        core, step = (k + 1) // 4, (k + 1) % 4
        target = place.device(x=place.along("x", step), c=place.c + core * (1 - 2 * place.c))
        place.send(landed.at[7], landed.at[k], target, slots[k])
    yield
    total = own
    for k in range(7):
        place.arrive(landed.at[k], slots[k])
        total = total + landed[k]
    tiles[place.z, place.y] = total
    slots = [place.slot() for _ in range(6)]
    for step in (1, 2, 3):
        place.send(here, here, place.device(y=place.along("y", step)), slots[step - 1])
    yield
    for step in (1, 2, 3):
        place.arrive(tiles.at[place.z, place.along("y", 4 - step)], slots[step - 1])
    for step in (1, 2, 3):
        place.send(tiles.at[place.z], tiles.at[place.z], place.device(z=place.along("z", step)), slots[2 + step])
    yield
    for step in (1, 2, 3):
        place.arrive(tiles.at[place.along("z", 4 - step)], slots[2 + step])
    table = tiles[...].reshape(128, 128).astype(BF16)
    row = lax.broadcasted_iota(jnp.int32, (128, 1), 0)
    z, y, core, x = row // 32, (row // 8) % 4, (row // 4) % 2, row % 4
    device = ((z // 2) * 64 + y * 16 + x * 4 + core * 2 + z % 2).astype(F32)
    for count, width, firsts in ((6, D, (0, 6)), (18, 3 * D, (12, 30, 48))):
        part, owner = remainder(lax.broadcasted_iota(jnp.int32, (1, width), 1), count)
        lane = lax.broadcasted_iota(jnp.int32, (128, 1), 0).astype(F32)
        for first in firsts:
            choose = jnp.where(lane - first == part, 1.0, 0.0).astype(BF16)
            spread_out = nn(table, choose)
            vector = jnp.sum(jnp.where(device == owner, spread_out, 0.0), axis=0, keepdims=True)
            base = first if count == 6 else first
            for k in range(width // 128):
                vec[base + k:base + k + 1, :] = vector[:, 128 * k:128 * (k + 1)]


def sum_vectors(place, vec, incoming):
    for stage, axis in enumerate("cxyz"):
        steps = (1,) if axis == "c" else (1, 2, 3)
        slots = [place.slot() for _ in steps]
        for k, step in enumerate(steps):
            device = place.device(c=1 - place.c) if axis == "c" else place.device(**{axis: place.along(axis, step)})
            place.send(vec.at[stage], incoming.at[stage, k], device, slots[k])
        yield
        total = vec[stage]
        for k, step in enumerate(steps):
            place.arrive(incoming.at[stage, k], slots[k])
            total = total + incoming[stage, k]
        vec[stage + 1] = total


def nt(left, right):
    return lax.dot_general(left, right, (((1,), (1,)), ((), ())), preferred_element_type=F32)


def tn(left, right):
    return lax.dot_general(left, right, (((0,), (0,)), ((), ())), preferred_element_type=F32)


def nn(left, right):
    return jnp.dot(left, right, preferred_element_type=F32)


def columns(ref, part, jp):
    halves = [ref[part, lax.rem(jp, 2), :, zl, :, :, lax.div(jp, 2)].reshape(D, 384) for zl in range(2)]
    return jnp.concatenate(halves, axis=1)


def put_columns(ref, part, jp, value):
    for zl in range(2):
        ref[part, lax.rem(jp, 2), :, zl, :, :, lax.div(jp, 2)] = (
            value[:, zl * 384:(zl + 1) * 384].astype(BF16).reshape(2, 4, 2, 48, 384)
        )


def row_pieces():
    return [(y, xh, xl, c) for y in range(2) for xh in range(2) for xl in range(2) for c in range(2)]


def rows(ref, jp):
    zh, y0 = lax.div(jp, 2), lax.rem(jp, 2) * 2
    halves = [
        jnp.concatenate([ref[2, c, zh, zl, y0 + y, xh, xl] for y, xh, xl, c in row_pieces()], axis=0) for zl in range(2)
    ]
    return jnp.concatenate(halves, axis=1)


def put_rows(ref, jp, value):
    zh, y0 = lax.div(jp, 2), lax.rem(jp, 2) * 2
    low = value.astype(BF16)
    for zl in range(2):
        for k, (y, xh, xl, c) in enumerate(row_pieces()):
            ref[2, c, zh, zl, y0 + y, xh, xl] = low[48 * k:48 * k + 48, zl * 384:(zl + 1) * 384]


def normalize(values):
    mean = jnp.mean(values, axis=-1, keepdims=True)
    centred = values - mean
    inverse = lax.rsqrt(jnp.mean(centred * centred, axis=-1, keepdims=True) + EPS)
    return centred * inverse, inverse


def norm_back(grad, normed, inverse):
    first = jnp.mean(grad, axis=-1, keepdims=True)
    second = jnp.mean(grad * normed, axis=-1, keepdims=True)
    return inverse * (grad - first - normed * second)


def shifted(values, steps):
    count = values.shape[0]
    row = lax.broadcasted_iota(jnp.int32, values.shape, 0)
    rolled = pltpu.roll(values, steps % count, 0)
    return jnp.where(row >= steps if steps > 0 else row < count + steps, rolled, 0.0)


def layer_kernel(tok, cot, wq, wo, wu, wd, ga, gf, taps, out, gtok, gq, go, gu, gd, gga, ggf, gtap, *scratch):
    (w, from_core, to_peer, from_peer, pile, down_s, down, few, tiles, few_landed, vec, prev, h1, n1, inv1, raw, mixed, bias,
     probs, att, h2, gh2, gatt, gqkv, gh1, acc, contrib, got, gvec, incoming, sums) = scratch[:31]
    lands, (send_sem, recv_sem) = scratch[31:-2], scratch[-2:]
    place = Place(send_sem, recv_sem)
    c, zl, rank = place.c, place.zl, place.zl
    ready = place.greet()
    for number in range(8):
        source = wq[:, number * 384:(number + 1) * 384] if number < 6 else wo[:, (number - 6) * 384:(number - 5) * 384]
        to_peer[number, 0, 0:6, :] = source.astype(F32)
        to_peer[number, 1, 0:6, :] = wu[:, number * 384:(number + 1) * 384].astype(F32)
    left, right = wd[:, 0:384].astype(F32), wd[:, 384:768].astype(F32)
    down_s[...] = jnp.where(zl == 0, right, left)
    down[pl.ds(pl.multiple_of(zl * 24, 8), 24), :] = jnp.where(zl == 0, left, right)
    few[...] = jnp.zeros_like(few)
    few[0:1, 0:6] = ga[...].astype(F32)
    few[0:1, 6:12] = gf[...].astype(F32)
    for j in range(3):
        few[0:1, 12 + 18 * j:30 + 18 * j] = taps[j:j + 1, :].astype(F32)
    few[...] = jnp.broadcast_to(few[0:1, :], (8, 128))
    vectors = gather_vectors(place, few, tiles, few_landed, vec)
    next(vectors)
    ready()

    other = place.device(z=place.flip(place.z, 1))
    trade = [place.slot() for _ in range(8)]
    _, mine = place.member(0)
    for d in range(1, 8):
        device, number = place.member(d)
        place.send(to_peer.at[number], from_peer.at[mine], device, trade[d])
    place.send(down_s, down.at[pl.ds(pl.multiple_of(zl * 24, 8), 24)], other, trade[0])
    next(vectors)
    from_peer[mine] = to_peer[mine]

    def normalize_half(half):
        normed, inverse = normalize((prev if half == 0 else tok)[...].astype(F32))
        here = pl.ds(half * ROWS, ROWS)
        n1[here, :] = normed
        inv1[here, :] = inverse

    for d in range(1, 8):
        _, number = place.member(d)
        place.arrive(from_peer.at[number], trade[d])
    place.arrive(down.at[pl.ds(pl.multiple_of((1 - zl) * 24, 8), 24)], trade[0])
    at = (c, lax.div(place.z, 2), zl, place.y, lax.div(place.x, 2), lax.rem(place.x, 2))
    for k in range(2):
        for number in range(8):
            pile[k, 6 * number:6 * number + 8, :] = from_peer[number, k]
        w[(k,) + at] = pile[k, 0:48, :].astype(BF16)
    w[(2,) + at] = down[...].astype(BF16)
    phase = [[gather_strip(place, w, part, sub) for sub in range(3)] for part in range(3)]
    advance(phase[0])
    next(vectors)
    token_slot, back_slot = place.slot(), place.slot()
    advance(phase[0])

    @pl.when(zl == 0)
    def _():
        place.copy(tok, prev, other, token_slot).start()

    next(vectors)
    advance(phase[1])
    normalize_half(1)
    advance(phase[0])
    next(vectors, None)
    advance(phase[1])
    advance(phase[2])
    advance(phase[0])
    advance(phase[1])
    advance(phase[2])

    @pl.when(zl == 1)
    def _():
        place.arrive(prev, token_slot)

    @pl.when(zl == 0)
    def _():
        prev[...] = jnp.zeros_like(prev)

    normalize_half(0)
    gain_one = jnp.concatenate([vec[r:r + 1, :] for r in range(6)], axis=1)
    gain_two = jnp.concatenate([vec[r:r + 1, :] for r in range(6, 12)], axis=1)
    h1[...] = (n1[...] * gain_one).astype(BF16)
    row = lax.broadcasted_iota(jnp.int32, (ROWS, EXT), 0)
    column = lax.broadcasted_iota(jnp.int32, (ROWS, EXT), 1)
    behind = jnp.where(column < ROWS, (1 - rank) * EXT, column - ROWS)
    bias[...] = jnp.where(behind <= row, 0.0, -1e30)
    first = lax.broadcasted_iota(jnp.int32, (ROWS, 128), 1) < 64
    gvec[0] = jnp.zeros((VEC, 128), F32)
    advance(phase[0])
    advance(phase[0])

    def tap(j, t):
        return vec[pl.ds(12 + TILES * j + t, 1), :]

    @pl.loop(0, 3)
    def _(jp):
        block = nn(h1[...], columns(w, 0, jp)).astype(BF16)
        for k in range(6):
            t = 6 * jp + k
            tile = block[:, 128 * k:128 * (k + 1)]
            raw[t] = tile
            value = tile.astype(F32)
            conv = tap(0, t) * value + tap(1, t) * shifted(value, 1) + tap(2, t) * shifted(value, 2)
            mixed[t] = conv.astype(BF16)

    def both(value):
        zero = jnp.zeros_like(value)
        return jnp.concatenate([jnp.where(first, value, zero), jnp.where(first, zero, value)], axis=0)

    def pick(value):
        return jnp.where(first, value[:ROWS], value[ROWS:])

    def attend(p):
        query = both(mixed[p, ROWS:, :])
        key, value = mixed[PAIRS + p], mixed[2 * PAIRS + p]
        scores = nt(query, key) * 0.125 + jnp.concatenate([bias[...], bias[...]], axis=0)
        weights = jnp.exp(scores - jnp.max(scores, axis=-1, keepdims=True))
        exact = weights * (1.0 / jnp.sum(weights, axis=-1, keepdims=True))
        probs[p] = exact
        att[p] = pick(nn(exact.astype(BF16), value)).astype(BF16)

    advance(phase[1])
    advance(phase[2])
    for p in range(PAIRS):
        attend(p)
        if p in (1, 3):
            advance(phase[1])
        if p in (2, 4):
            advance(phase[2])

    attended = jnp.concatenate([att[p] for p in range(PAIRS)], axis=1)
    resid = tok[...].astype(F32) + nn(attended, columns(w, 0, 3))
    normed_two, inverse_two = normalize(resid)
    h2[...] = (normed_two * gain_two).astype(BF16)
    acc[...] = resid
    gh2[...] = jnp.zeros_like(gh2)
    for _ in range(6):
        advance(phase[1])
        advance(phase[2])
    place.drain()

    @pl.when(zl == 0)
    def _():
        place.copy(tok, tok, other, token_slot).wait_send()

    @pl.loop(0, 4)
    def _(jp):
        up = columns(w, 1, jp)
        low = rows(w, jp)
        rect = jnp.maximum(nn(h2[...], up), 0.0)
        act = (rect * rect).astype(BF16)
        acc[...] += nn(act, low)
        gact = nt(cot[...], low)
        gup = (gact * 2.0 * rect).astype(BF16)
        gh2[...] += nt(gup, up)
        put_rows(w, jp, tn(act, cot[...]))
        put_columns(w, 1, jp, tn(h2[...], gup))

    sent = {part: [scatter_strip(place, w, part, sub, from_core, lands[15 * part + 5 * sub:15 * part + 5 * sub + 5], sums) for sub in range(3)] for part in range(3)}
    advance(sent[2])
    advance(sent[1])
    out[...] = acc[...].astype(BF16)
    grad_two = gh2[...]
    summed = jnp.sum(grad_two * normed_two, axis=0, keepdims=True)
    for r in range(6):
        gvec[0, 6 + r:7 + r, :] = summed[:, 128 * r:128 * (r + 1)]
    grad_resid = cot[...].astype(F32) + norm_back(grad_two * gain_two, normed_two, inverse_two)
    acc[...] = grad_resid
    gproj = grad_resid.astype(BF16)
    gback = nt(gproj, columns(w, 0, 3)).astype(BF16)
    for p in range(PAIRS):
        gatt[p] = gback[:, 128 * p:128 * (p + 1)]
    advance(sent[2])
    put_columns(w, 0, 3, tn(attended, gproj))

    def attend_back(p):
        query = both(mixed[p, ROWS:, :])
        key, value = mixed[PAIRS + p], mixed[2 * PAIRS + p]
        grad = both(gatt[p])
        exact = probs[p]
        gvalue = tn(exact.astype(BF16), grad)
        gprobs = nt(grad, value)
        centred = gprobs - jnp.sum(gprobs * exact, axis=-1, keepdims=True)
        gscores = (exact * centred).astype(BF16)
        gquery = pick(nn(gscores, key)) * 0.125
        gkey = tn(gscores, query) * 0.125
        for k, tile in enumerate((jnp.concatenate([jnp.zeros_like(gquery), gquery], axis=0), gkey, gvalue)):
            t = PAIRS * k + p
            back = tap(0, t) * tile + tap(1, t) * shifted(tile, -1) + tap(2, t) * shifted(tile, -2)
            gqkv[t] = back.astype(BF16)
            value_in = raw[t].astype(F32)
            for j in range(3):
                delayed = value_in if j == 0 else shifted(value_in, j)
                gvec[0, pl.ds(12 + TILES * j + t, 1), :] = jnp.sum(tile * delayed, axis=0, keepdims=True)

    for p in range(PAIRS):
        attend_back(p)
        advance(sent[1] if p % 2 == 0 else sent[2])

    gh1[...] = jnp.zeros_like(gh1)

    @pl.loop(0, 3)
    def _(jp):
        grad = jnp.concatenate([gqkv[6 * jp + k] for k in range(6)], axis=1)
        gh1[...] += nt(grad, columns(w, 0, jp))
        put_columns(w, 0, jp, tn(h1[...], grad))

    advance(sent[0])
    total = jnp.zeros((1, D), F32)
    for half in range(2):
        here = pl.ds(half * ROWS, ROWS)
        grad_one = gh1[here, :]
        total = total + jnp.sum(grad_one * n1[here, :], axis=0, keepdims=True)
        back = norm_back(grad_one * gain_one, n1[here, :], inv1[here, :])
        if half == 0:
            contrib[...] = back.astype(BF16)

            @pl.when(zl == 1)
            def _():
                place.copy(contrib, got, other, back_slot).start()
        else:
            acc[...] += back
    for r in range(6):
        gvec[0, r:r + 1, :] = total[:, 128 * r:128 * (r + 1)]
    advance(sent[0])
    for _ in range(6):
        advance(sent[1])
        advance(sent[2])
    small = sum_vectors(place, gvec, incoming)
    for _ in range(5):
        next(small, None)
        advance(sent[0])

    for number in range(8):
        for k in range(2):
            to_peer[number, k, 0:6, :] = sums[k, 6 * number:6 * number + 6, :]
    trade = [place.slot() for _ in range(8)]
    back_from = pile.at[0, pl.ds(0, 24)]
    arrived = from_core_free = from_peer
    for d in range(1, 8):
        device, number = place.member(d)
        place.send(to_peer.at[number], arrived.at[mine], device, trade[d])
    place.send(sums.at[2, pl.ds(pl.multiple_of((1 - zl) * 24, 8), 24)], back_from, other, trade[0])
    arrived[mine] = to_peer[mine]
    summed = gvec[4]
    gains = [jnp.concatenate([summed[r:r + 1] for r in range(6 * k, 6 * k + 6)], axis=1) for k in range(2)]
    tapped = [jnp.concatenate([summed[r:r + 1] for r in range(12 + TILES * j, 12 + TILES * j + TILES)], axis=1) for j in range(3)]
    gain_rows = jnp.concatenate(gains + [jnp.zeros((6, D), F32)], axis=0)
    tap_rows = jnp.concatenate(tapped + [jnp.zeros((5, 3 * D), F32)], axis=0)
    exactly = functools.partial(
        lax.dot_general,
        dimension_numbers=(((1,), (1,)), ((), ())),
        preferred_element_type=F32,
        precision=lax.Precision.HIGHEST,
    )
    gain_own = exactly(gain_rows, spread(place.index, 6, D))
    gga[...] = gain_own[0:1, 0:6]
    ggf[...] = gain_own[1:2, 0:6]
    gtap[...] = exactly(tap_rows, spread(place.index, 18, 3 * D))[0:3, 0:18]

    @pl.when(zl == 0)
    def _():
        place.arrive(got, back_slot)

    @pl.when(zl == 1)
    def _():
        got[...] = jnp.zeros_like(got)

    gtok[...] = (acc[...] + got[...].astype(F32)).astype(BF16)
    for d in range(1, 8):
        _, number = place.member(d)
        place.arrive(arrived.at[number], trade[d])
    place.arrive(back_from, trade[0])
    for number in range(8):
        if number < 6:
            gq[:, 384 * number:384 * (number + 1)] = arrived[number, 0, 0:6, :]
        else:
            go[:, 384 * (number - 6):384 * (number - 5)] = arrived[number, 0, 0:6, :]
        gu[:, 384 * number:384 * (number + 1)] = arrived[number, 1, 0:6, :]
    own = sums[2, pl.ds(pl.multiple_of(zl * 24, 8), 24), :]
    theirs = pile[0, 0:24, :]
    gd[:, 0:384] = jnp.where(zl == 0, own, theirs)
    gd[:, 384:768] = jnp.where(zl == 0, theirs, own)
    place.drain()

    @pl.when(zl == 1)
    def _():
        place.copy(contrib, contrib, other, back_slot).wait_send()


def kept(axes):
    grid = []
    for axis in "zyx":
        if axis not in axes:
            grid += {"z": [2, 2], "y": [4], "x": [2, 2]}[axis]
    return tuple(grid)


RESULTS = (
    ((ROWS, D), BF16),
    ((ROWS, D), BF16),
    ((6, 2304), F32),
    ((6, 768), F32),
    ((6, 3072), F32),
    ((24, 768), F32),
    ((1, 6), F32),
    ((1, 6), F32),
    ((3, 18), F32),
)


def layer(*args):
    vmem = pl.BlockSpec(memory_space=pltpu.VMEM)
    lands = []
    for _ in range(3):
        for sub in range(3):
            order = BACK[sub]
            grids = [(2,) + HALVES[order[0]], kept(order[:1]), kept(order[:1]), (3,) + kept(order[:2]), (3,)]
            lands += [pltpu.VMEM(grid + (16, 384), BF16) for grid in grids]
    return pl.pallas_call(
        layer_kernel,
        out_shape=tuple(jax.ShapeDtypeStruct(*result) for result in RESULTS),
        in_specs=[vmem] * 9,
        out_specs=(vmem,) * 9,
        scratch_shapes=[
            pltpu.VMEM((3,) + GRID + BLOCK, BF16),
            pltpu.VMEM((3,) + GRID[1:] + BLOCK, BF16),
            pltpu.VMEM((8, 2, 8, 384), F32),
            pltpu.VMEM((8, 2, 8, 384), F32),
            pltpu.VMEM((2, 56, 384), F32),
            pltpu.VMEM((24, 384), F32),
            pltpu.VMEM((48, 384), F32),
            pltpu.VMEM((8, 128), F32),
            pltpu.VMEM((4, 4, 8, 128), F32),
            pltpu.VMEM((8, 8, 128), F32),
            pltpu.VMEM((VEC, 128), F32),
            pltpu.VMEM((ROWS, D), BF16),
            pltpu.VMEM((EXT, D), BF16),
            pltpu.VMEM((EXT, D), F32),
            pltpu.VMEM((EXT, 1), F32),
            pltpu.VMEM((TILES, EXT, 128), BF16),
            pltpu.VMEM((TILES, EXT, 128), BF16),
            pltpu.VMEM((ROWS, EXT), F32),
            pltpu.VMEM((PAIRS, EXT, EXT), F32),
            pltpu.VMEM((PAIRS, ROWS, 128), BF16),
            pltpu.VMEM((ROWS, D), BF16),
            pltpu.VMEM((ROWS, D), F32),
            pltpu.VMEM((PAIRS, ROWS, 128), BF16),
            pltpu.VMEM((TILES, EXT, 128), BF16),
            pltpu.VMEM((EXT, D), F32),
            pltpu.VMEM((ROWS, D), F32),
            pltpu.VMEM((ROWS, D), BF16),
            pltpu.VMEM((ROWS, D), BF16),
            pltpu.VMEM((5, VEC, 128), F32),
            pltpu.VMEM((4, 3, VEC, 128), F32),
            pltpu.VMEM((3,) + BLOCK, F32),
            *lands,
            pltpu.SemaphoreType.DMA((340,)),
            pltpu.SemaphoreType.DMA((340,)),
        ],
        compiler_params=pltpu.CompilerParams(collective_id=0, has_side_effects=True, vmem_limit_bytes=LIMIT),
    )(*args)


def copy_kernel(*refs):
    count = len(RESULTS)
    copies = [pltpu.make_async_copy(refs[k], refs[count + k], refs[-1].at[k]) for k in range(count)]
    for copy in copies:
        copy.start()
    for copy in copies:
        copy.wait()


def copied(*args):
    anywhere = pl.BlockSpec(memory_space=pl.ANY)
    return pl.pallas_call(
        copy_kernel,
        out_shape=tuple(jax.ShapeDtypeStruct(*result) for result in RESULTS),
        in_specs=[anywhere] * len(RESULTS),
        out_specs=(anywhere,) * len(RESULTS),
        scratch_shapes=[pltpu.SemaphoreType.DMA((len(RESULTS),))],
    )(*args)


def per_device(tokens, w_qkv, w_out, w_up, w_down, gain_attn, gain_ffn, conv_taps, cotangent):
    results = copied(*layer(
        tokens, cotangent, w_qkv, w_out, w_up, w_down, gain_attn.reshape(1, 6), gain_ffn.reshape(1, 6), conv_taps
    ))
    return results[:6] + (results[6].reshape(6), results[7].reshape(6), results[8])


def solution(mesh):
    both = ("grp", "seq")
    row, one, column = P(both, None), P(both), P(None, both)
    return jax.shard_map(
        per_device,
        mesh=mesh,
        in_specs=(row, row, row, row, row, one, one, column, row),
        out_specs=(row, row, row, row, row, row, one, one, column),
        check_vma=False,
    )
```

time: 198 us -> 173 us (0.87)
  Pallas kernels: 186 us -> 172 us
  local copies, waits for them, and re-layouts: 11.3 us -> 0 us
    pallas_call x3 -> x2, Pallas kernels: 186 us -> 172 us  [the longest x1 139 us: layer(): pl.pallas_call(layer_kernel, out_shape=tuple((jax.ShapeDtypeStruct(*resul...]
    unnamed x8 -> x0, local copies, waits for them, and re-layouts: 11.3 us -> none
where the time goes in v2:
time: 173 us
  Pallas kernels  172 us (99%)
    pallas_call x1, Pallas kernels, layer(): pl.pallas_call(layer_kernel, out_shape=tuple((jax.ShapeDtypeStruct(*resul...  139 us
    pallas_call x1, Pallas kernels, copied(): pl.pallas_call(copy_kernel, out_shape=tuple((jax.ShapeDtypeStruct(*result...  33.3 us

profile of v2, /device:TPU:1, one launch (start us, length us, event | category | flops | bytes accessed | tf_op | source)
XLA Modules:
  0.0 172.8 jit_solution(4041649895168117397)
XLA Ops:
  0.6 138.6 %shard_map.160 = (bf16[256,768]{1,0:T(8,128)(2,1)}, bf16[256,768]{1,0:T(8,128)(2,1)}, f32[6,2304]{1,0:T(8,128)}, f32[6,768]{1,0:T(8,128)}, f32[6,3072]{1,0:T(8,1...) custom-call(bf16[256,768]{1,0:T(8,128)(2,1)} %tok.1, bf16[256,768]{1,0:T(8,128)(2,1)} %cot.1, ...), custom_call_target="tpu_custom_call" | custom-call | tf_op jit(solution)/shard_map/pallas_call | solution.py:687
  139.3 33.3 %shard_map.161 = (bf16[256,768]{1,0:T(8,128)(2,1)}, bf16[256,768]{1,0:T(8,128)(2,1)}, f32[6,2304]{1,0:T(8,128)}, f32[6,768]{1,0:T(8,128)}, f32[6,3072]{1,0:T(8,1...) custom-call(bf16[256,768]{1,0:T(8,128)(2,1)} %get-tuple-element.27.refs_0_, ...), custom_call_target="tpu_custom_call" | custom-call | tf_op jit(solution)/shard_map/pallas_call | solution.py:743

commit v3 on v2

v3 whole, which is shorter than its diff:
```python
import functools

import jax
import jax.numpy as jnp
from jax import lax
from jax.experimental import pallas as pl
from jax.experimental.pallas import tpu as pltpu
from jax.sharding import PartitionSpec as P

MESH = pl.DeviceIdType.MESH
F32 = jnp.float32
BF16 = jnp.bfloat16
EPS = 1e-05
D = 768
ROWS = 256
EXT = 512
PAIRS = 6
TILES = 18
BLOCK = (48, 384)
GRID = (2, 2, 2, 4, 2, 2)
VEC = 80
ORDERS = (("x", "y", "z"), ("y", "z", "x"), ("z", "x", "y"))
BACK = (("z", "y", "x"), ("x", "z", "y"), ("y", "x", "z"))
LIMIT = 60 * 2**20
READY = tuple(range(18, 24)) + tuple(t for p in range(6) for t in (p, 6 + p, 12 + p))
CHUNKS = ((0, 256), (256, 128))

LEAN_IN = (False, True, True)
LEAN_OUT = (True, True, True)


class Place:
    def __init__(self, send_sem, recv_sem):
        grp, seq = lax.axis_index("grp"), lax.axis_index("seq")
        self.c = lax.rem(grp, 2)
        self.x = lax.rem(lax.div(grp, 2), 4)
        self.y = lax.rem(lax.div(grp, 8), 4)
        self.z = lax.div(grp, 32) * 2 + seq
        self.zl = seq
        self.index = grp * 2 + seq
        self.send_sem, self.recv_sem = send_sem, recv_sem
        self.sends = self.receives = 0
        self.owed = []

    def device(self, **new):
        at = {"x": self.x, "y": self.y, "z": self.z, "c": self.c}
        at.update(new)
        grp = ((lax.div(at["z"], 2) * 4 + at["y"]) * 4 + at["x"]) * 2 + at["c"]
        return (grp, lax.rem(at["z"], 2))

    def along(self, axis, delta):
        return lax.rem(getattr(self, axis) + delta, 4)

    def flip(self, value, bit):
        return value + bit * (1 - 2 * lax.rem(value, 2))

    def member(self, d):
        x, c, z = self.flip(self.x, d // 4), self.flip(self.c, (d // 2) % 2), self.flip(self.z, d % 2)
        number = lax.rem(x, 2) * 4 + c * 2 + lax.rem(z, 2)
        return self.device(x=x, c=c, z=z), number

    def greet(self):
        barrier = pltpu.get_barrier_semaphore()
        partners = [self.device(**{a: self.along(a, d)}) for a in "xyz" for d in (1, 2, 3)]
        partners += [self.member(d)[0] for d in (2, 3, 5, 6, 7)]
        for partner in partners:
            pl.semaphore_signal(barrier, inc=1, device_id=partner, device_id_type=MESH)
        return lambda: pl.semaphore_wait(barrier, len(partners))

    def slot(self, count=1):
        self.receives += count
        return self.receives - count

    def outbox(self, *wholes):
        self.sends += 1
        self.owed.append((self.sends - 1, wholes))
        return self.sends - 1

    def copy(self, src, dst, device, out, slot):
        return pltpu.make_async_remote_copy(
            src_ref=src,
            dst_ref=dst,
            send_sem=self.send_sem.at[out],
            recv_sem=self.recv_sem.at[slot],
            device_id=device,
            device_id_type=MESH,
        )

    def send(self, src, dst, device, out, slot):
        self.copy(src, dst, device, out, slot).start()

    def arrive(self, whole, slot):
        self.copy(whole, whole, self.device(), 0, slot).wait_recv()

    def drain(self):
        for out, wholes in self.owed:
            for whole in wholes:
                self.copy(whole, whole, self.device(), out, 0).wait_send()
        self.owed = []


def spot(lead, c=None, tail=(), **at):
    index = list(lead) + [slice(None) if c is None else c]
    for axis in "zyx":
        value = at.get(axis)
        half = isinstance(value, tuple)
        if axis == "y":
            index.append(pl.ds(2 * value[1], 2) if half else slice(None) if value is None else value)
        elif half:
            index += [value[1], slice(None)]
        elif value is None:
            index += [slice(None), slice(None)]
        else:
            index += [lax.div(value, 2), lax.rem(value, 2)]
    return tuple(index) + tail


def strip(sub):
    return (pl.ds(16 * sub, 16), slice(None))


def spread(index, count, width):
    row = lax.broadcasted_iota(jnp.int32, (128, width), 0)
    column = lax.broadcasted_iota(jnp.int32, (128, width), 1)
    return jnp.where((column == count * index + row) & (row < count), 1.0, 0.0)


def gather_phase(place, w, part, lean):
    c = place.c
    here = {"x": place.x, "y": place.y, "z": place.z}
    sibling = place.device(c=1 - c)
    blocks = {3: w.at[part, 0, 0, 0, 0:3, 0, 0], 12: w.at[part, 0, 0, 0, 0:3], 16: w.at[part, 0, 0, 0], 48: w.at[part, 0, :, :, 0:3], 64: w.at[part, 0]}
    passing, passed = place.outbox(blocks[64]), place.slot()

    def piece(sub, **at):
        return w.at[spot((part,), c, strip(sub), **at)]

    def pass_on(sub, **at):
        place.send(piece(sub, **at), piece(sub, **at), sibling, passing, passed)

    for stage, count in ((0, 3), (1, 12)):
        out, slot = place.outbox(blocks[count]), place.slot()
        for sub in range(3):
            axis, done = ORDERS[sub][stage], ORDERS[sub][:stage]
            own = piece(sub, **{a: here[a] for a in "xyz" if a not in done})
            for step in (1, 2, 3):
                place.send(own, own, place.device(**{axis: place.along(axis, step)}), out, slot)
        yield
        place.arrive(blocks[count], slot)
    out, sides, last = place.outbox(blocks[48]), place.slot(6), place.slot()

    def toward(axis, side):
        return place.device(**{axis: place.along(axis, 3 if side else 1)})

    for sub in range(3):
        axis = ORDERS[sub][2]
        own = piece(sub, **{axis: here[axis]})
        for side in range(2):
            place.send(own, own, toward(axis, side), out, sides + 2 * sub + side)
    for sub in range(3):
        axis = ORDERS[sub][2]
        pass_on(sub, **{axis: here[axis]})
    yield
    for side in range(2):
        for sub in range(3):
            axis, whole = ORDERS[sub][2], ORDERS[sub][0]
            came = {axis: place.along(axis, 1 if side else 3)}
            place.arrive(piece(sub, **came), sides + 2 * sub + side)
            down_only = lean and axis == "z"
            if not down_only or side == 1:
                half = piece(sub, **came) if down_only else piece(sub, **came, **{whole: ("half", side)})
                place.send(half, half, toward(axis, side), out, last)
            pass_on(sub, **came)
    yield
    place.arrive(blocks[16], last)
    for sub in range(3):
        axis = ORDERS[sub][2]
        pass_on(sub, **{axis: place.along(axis, 2)})
    yield
    place.arrive(blocks[64], passed)


HALF = {"z": "y", "x": "z", "y": "x"}
HALVES = {"z": (2, 2, 2), "x": (2, 4), "y": (2, 2, 2)}


def half_of(axis, h):
    return {"z": (pl.ds(2 * h, 2),), "x": (h,), "y": (slice(None), slice(None), h)}[axis]


def scatter_phase(place, g, lead, tails, arrivals, landed, lands, finish, relayed, lean):
    c = place.c
    here = {"x": place.x, "y": place.y, "z": place.z}
    tail = (slice(None), tails[0][1])
    corner = lead + (0, 0, 0)
    blocks = {
        3: g.at[corner + (pl.ds(0, 3), 0, 0) + tail],
        12: g.at[corner + (pl.ds(0, 3), slice(None), slice(None)) + tail],
        48: g.at[lead + (0, slice(None), slice(None), pl.ds(0, 3), slice(None), slice(None)) + tail],
    }

    def at(sub, **where):
        return spot(lead, c, tails[sub], **where)

    for index, slot in arrivals:
        place.arrive(landed.at[index], slot)
        g[lead + (c,) + index] = g[lead + (c,) + index] + landed[index]
    out = place.outbox(blocks[48])

    def ways(sub):
        axis = BACK[sub][0]
        way = [(t, place.device(**{axis: t})) for t in (place.along(axis, 1), place.along(axis, 3))]
        return axis, HALF[axis], way, (0, 0) if lean and axis == "z" else (0, 1)

    if relayed:
        relays, sides = place.slot(6), place.slot(3)
        for sub in range(3):
            axis, whole, way, course = ways(sub)
            across = place.along(axis, 2)
            for k in range(2):
                src = g.at[at(sub, **{axis: across, whole: ("half", k)})]
                place.send(src, lands[sub][0].at[k], way[course[k]][1], out, relays + 2 * sub + k)
        for sub in range(3):
            axis, whole, way, course = ways(sub)
            for k in range(2):
                toward = 1 - course[k]
                coordinate, device = way[toward]
                src = g.at[at(sub, **{axis: coordinate, whole: ("half", k)})]
                place.send(src, lands[sub][1].at[(toward,) + half_of(axis, k)], device, out, sides + sub)
        yield
        for sub in range(3):
            axis, whole, way, course = ways(sub)
            relay, side = lands[sub][:2]
            for k in range(2):
                coordinate, device = way[course[k]]
                place.arrive(relay.at[k], relays + 2 * sub + k)
                index = at(sub, **{axis: coordinate, whole: ("half", k)})
                g[index] = g[index] + relay[k]
                place.send(g.at[index], side.at[(course[k],) + half_of(axis, k)], device, out, sides + sub)
        yield
    else:
        sides = place.slot(3)
        for step in (2, 1, 3):
            for sub in range(3):
                axis = BACK[sub][0]
                there = place.along(axis, step)
                src = g.at[at(sub, **{axis: there})]
                place.send(src, lands[sub][1].at[step - 1], place.device(**{axis: there}), out, sides + sub)
        yield
    out, slot = place.outbox(blocks[12]), place.slot()
    for sub in range(3):
        axis, second = BACK[sub][0], BACK[sub][1]
        side = lands[sub][1]
        place.arrive(side, sides + sub)
        index = at(sub, **{axis: here[axis]})
        total = g[index].astype(F32)
        for k in range(side.shape[0]):
            total = total + side[k].astype(F32)
        g[index] = total.astype(BF16)
        for step in (1, 2, 3):
            there = place.along(second, step)
            src = g.at[at(sub, **{axis: here[axis], second: there})]
            place.send(src, lands[sub][2].at[step - 1], place.device(**{second: there}), out, slot)
    yield
    place.arrive(blocks[12], slot)
    out, slot = place.outbox(blocks[3]), place.slot()
    for sub in range(3):
        own = {a: here[a] for a in BACK[sub][:2]}
        third = BACK[sub][2]
        index = at(sub, **own)
        total = g[index].astype(F32)
        for step in range(3):
            total = total + lands[sub][2][step].astype(F32)
        g[index] = total.astype(BF16)
        for step in (1, 2, 3):
            there = place.along(third, step)
            src = g.at[at(sub, **own, **{third: there})]
            place.send(src, lands[sub][3].at[step - 1], place.device(**{third: there}), out, slot)
    yield
    place.arrive(blocks[3], slot)
    for sub in range(3):
        total = g[at(sub, **here)].astype(F32)
        for step in range(3):
            total = total + lands[sub][3][step].astype(F32)
        finish(sub, total)


def advance(*steps):
    for step in steps:
        next(step, None)


def remainder(value, count):
    value = value.astype(F32)
    whole = jnp.floor((value + 0.5) * (1.0 / count))
    return value - whole * count, whole


def gather_vectors(place, few, tiles, landed, vec):
    sublane = lax.broadcasted_iota(jnp.int32, (8, 128), 0)
    mine = place.c * 4 + place.x
    landed[3] = jnp.where(sublane == mine, few[...], 0.0)
    yield
    out, slot = place.outbox(landed.at[0:3]), place.slot()
    for step in (1, 2, 3):
        place.send(landed.at[3], landed.at[step - 1], place.device(x=place.along("x", step)), out, slot)
    yield
    place.arrive(landed.at[0:3], slot)
    landed[4] = landed[0] + landed[1] + landed[2] + landed[3]
    out, slot = place.outbox(landed.at[4]), place.slot()
    place.send(landed.at[4], landed.at[5], place.device(c=1 - place.c), out, slot)
    yield
    place.arrive(landed.at[5], slot)
    tiles[place.z, place.y] = landed[4] + landed[5]
    here = tiles.at[place.z, place.y]
    out, slot = place.outbox(landed.at[0:3]), place.slot()
    for step in (1, 2, 3):
        place.send(here, here, place.device(y=place.along("y", step)), out, slot)
    yield
    place.arrive(landed.at[0:3], slot)
    out, slot = place.outbox(tiles.at[0:3]), place.slot()
    for step in (1, 2, 3):
        place.send(tiles.at[place.z], tiles.at[place.z], place.device(z=place.along("z", step)), out, slot)
    yield
    place.arrive(tiles.at[0:3], slot)
    table = tiles[...].reshape(128, 128).astype(BF16)
    row = lax.broadcasted_iota(jnp.int32, (128, 1), 0)
    z, y, core, x = row // 32, (row // 8) % 4, (row // 4) % 2, row % 4
    device = ((z // 2) * 64 + y * 16 + x * 4 + core * 2 + z % 2).astype(F32)
    for count, width, firsts in ((6, D, (0, 6)), (18, 3 * D, (12, 30, 48))):
        part, owner = remainder(lax.broadcasted_iota(jnp.int32, (1, width), 1), count)
        lane = lax.broadcasted_iota(jnp.int32, (128, 1), 0).astype(F32)
        for first in firsts:
            choose = jnp.where(lane - first == part, 1.0, 0.0).astype(BF16)
            spread_out = nn(table, choose)
            vector = jnp.sum(jnp.where(device == owner, spread_out, 0.0), axis=0, keepdims=True)
            base = first if count == 6 else first
            for k in range(width // 128):
                vec[base + k:base + k + 1, :] = vector[:, 128 * k:128 * (k + 1)]


def sum_vectors(place, vec, incoming):
    for stage, axis in enumerate("cxyz"):
        steps = (1,) if axis == "c" else (1, 2, 3)
        whole = incoming.at[stage, 0:len(steps)]
        out, slot = place.outbox(whole), place.slot()
        for k, step in enumerate(steps):
            device = place.device(c=1 - place.c) if axis == "c" else place.device(**{axis: place.along(axis, step)})
            place.send(vec.at[stage], incoming.at[stage, k], device, out, slot)
        yield
        place.arrive(whole, slot)
        total = vec[stage]
        for k in range(len(steps)):
            total = total + incoming[stage, k]
        vec[stage + 1] = total


def nt(left, right):
    return lax.dot_general(left, right, (((1,), (1,)), ((), ())), preferred_element_type=F32)


def tn(left, right):
    return lax.dot_general(left, right, (((0,), (0,)), ((), ())), preferred_element_type=F32)


def nn(left, right):
    return jnp.dot(left, right, preferred_element_type=F32)


def columns(ref, part, jp):
    halves = [ref[part, lax.rem(jp, 2), :, zl, :, :, lax.div(jp, 2)].reshape(D, 384) for zl in range(2)]
    return jnp.concatenate(halves, axis=1)


def tile_at(t):
    j, q = READY.index(t) % 8, READY.index(t) // 8
    xl, c, zl = j // 4, j // 2 % 2, j % 2
    every = slice(None)
    return (c, every, zl, every, every, xl, every, pl.ds(128 * q, 128))


def tiles_of(w, wanted):
    return jnp.concatenate([w[(0,) + tile_at(t)].reshape(D, 128) for t in wanted], axis=1)


def put_tiles(g, wanted, value):
    low = value.astype(BF16)
    for k, t in enumerate(wanted):
        g[tile_at(t)] = low[:, 128 * k:128 * (k + 1)].reshape(2, 4, 2, 48, 128)


def put_columns(ref, part, jp, value):
    for zl in range(2):
        ref[part, lax.rem(jp, 2), :, zl, :, :, lax.div(jp, 2)] = (
            value[:, zl * 384:(zl + 1) * 384].astype(BF16).reshape(2, 4, 2, 48, 384)
        )


def row_pieces():
    return [(y, xh, xl, c) for y in range(2) for xh in range(2) for xl in range(2) for c in range(2)]


def rows(ref, jp):
    zh, y0 = lax.div(jp, 2), lax.rem(jp, 2) * 2
    halves = [
        jnp.concatenate([ref[2, c, zh, zl, y0 + y, xh, xl] for y, xh, xl, c in row_pieces()], axis=0) for zl in range(2)
    ]
    return jnp.concatenate(halves, axis=1)


def put_rows(ref, jp, value):
    zh, y0 = lax.div(jp, 2), lax.rem(jp, 2) * 2
    low = value.astype(BF16)
    for zl in range(2):
        for k, (y, xh, xl, c) in enumerate(row_pieces()):
            ref[2, c, zh, zl, y0 + y, xh, xl] = low[48 * k:48 * k + 48, zl * 384:(zl + 1) * 384]


def normalize(values):
    mean = jnp.mean(values, axis=-1, keepdims=True)
    centred = values - mean
    inverse = lax.rsqrt(jnp.mean(centred * centred, axis=-1, keepdims=True) + EPS)
    return centred * inverse, inverse


def norm_back(grad, normed, inverse):
    first = jnp.mean(grad, axis=-1, keepdims=True)
    second = jnp.mean(grad * normed, axis=-1, keepdims=True)
    return inverse * (grad - first - normed * second)


def shifted(values, steps):
    count = values.shape[0]
    row = lax.broadcasted_iota(jnp.int32, values.shape, 0)
    rolled = pltpu.roll(values, steps % count, 0)
    return jnp.where(row >= steps if steps > 0 else row < count + steps, rolled, 0.0)


def layer_kernel(tok, cot, wq, wo, wu, wd, ga, gf, taps, out, gtok, gq, go, gu, gd, gga, ggf, gtap, *scratch):
    (w, g0, h1t, h2t, from_core, to_peer, from_peer, pile, down_s, down, few, tiles, few_landed, vec, prev, h1, raw, mixed, bias,
     probs, att, h2, act, gup, gh2, gatt, acc, contrib, got, gvec, incoming, sums) = scratch[:32]
    lands, (send_sem, recv_sem) = scratch[32:-2], scratch[-2:]
    place = Place(send_sem, recv_sem)
    c, zl, rank = place.c, place.zl, place.zl
    ready = place.greet()
    for number in range(8):
        for q in range(3):
            t = READY[8 * q + number]
            source = wq[:, t * 128:(t + 1) * 128] if t < 18 else wo[:, (t - 18) * 128:(t - 17) * 128]
            to_peer[0, number, 0:6, q * 128:(q + 1) * 128] = source.astype(F32)
        to_peer[1, number, 0:6, :] = wu[:, number * 384:(number + 1) * 384].astype(F32)
    left, right = wd[:, 0:384].astype(F32), wd[:, 384:768].astype(F32)
    down_s[...] = jnp.where(zl == 0, right, left)
    down[pl.ds(pl.multiple_of(zl * 24, 8), 24), :] = jnp.where(zl == 0, left, right)
    few[...] = jnp.zeros_like(few)
    few[0:1, 0:6] = ga[...].astype(F32)
    few[0:1, 6:12] = gf[...].astype(F32)
    for j in range(3):
        few[0:1, 12 + 18 * j:30 + 18 * j] = taps[j:j + 1, :].astype(F32)
    few[...] = jnp.broadcast_to(few[0:1, :], (8, 128))
    vectors = gather_vectors(place, few, tiles, few_landed, vec)
    advance(vectors)
    ready()

    other = place.device(z=place.flip(place.z, 1))
    trades, trade_down, token_slot, back_slot = place.slot(2), place.slot(), place.slot(), place.slot()
    out_trades, out_down = [place.outbox(from_peer.at[0, 0:7]) for _ in range(2)], place.outbox(down_s)
    out_tokens = place.outbox()
    _, mine = place.member(0)
    def trade(k):
        for d in range(1, 8):
            device, number = place.member(d)
            place.send(to_peer.at[k, number], from_peer.at[k, mine], device, out_trades[k], trades + k)

    trade(0)
    trade(1)
    place.send(down_s, down.at[pl.ds(pl.multiple_of(zl * 24, 8), 24)], other, out_down, trade_down)
    next(vectors)

    for k in range(2):
        from_peer[k, mine] = to_peer[k, mine]

    def normalize_half(half):
        return normalize((prev if half == 0 else tok)[...].astype(F32))

    place.arrive(down_s, trade_down)
    at = (c, lax.div(place.z, 2), zl, place.y, lax.div(place.x, 2), lax.rem(place.x, 2))
    for k in range(2):
        place.arrive(from_peer.at[k, 0:7], trades + k)
        for number in range(8):
            pile[k, 6 * number:6 * number + 8, :] = from_peer[k, number]
        w[(k,) + at] = pile[k, 0:48, :].astype(BF16)
    w[(2,) + at] = down[...].astype(BF16)
    phase = [gather_phase(place, w, part, LEAN_IN[part]) for part in range(3)]
    advance(vectors)
    for _ in range(3):
        advance(*phase)
        advance(vectors)

    @pl.when(zl == 0)
    def _():
        place.send(tok, prev, other, out_tokens, token_slot)

    advance(*phase)

    @pl.when(zl == 1)
    def _():
        place.arrive(prev, token_slot)

    @pl.when(zl == 0)
    def _():
        prev[...] = jnp.zeros_like(prev)

    gain_one = jnp.concatenate([vec[r:r + 1, :] for r in range(6)], axis=1)
    gain_two = jnp.concatenate([vec[r:r + 1, :] for r in range(6, 12)], axis=1)
    for half in range(2):
        h1[half * ROWS:(half + 1) * ROWS, :] = (normalize_half(half)[0] * gain_one).astype(BF16)
    h1t[...] = h1[...].T
    row = lax.broadcasted_iota(jnp.int32, (ROWS, EXT), 0)
    column = lax.broadcasted_iota(jnp.int32, (ROWS, EXT), 1)
    behind = jnp.where(column < ROWS, (1 - rank) * EXT, column - ROWS)
    bias[...] = jnp.where(behind <= row, 0.0, -1e30)
    first = lax.broadcasted_iota(jnp.int32, (ROWS, 128), 1) < 64
    gvec[0] = jnp.zeros((VEC, 128), F32)
    advance(*phase)
    advance(phase[0])

    def tap(j, t):
        return vec[pl.ds(12 + TILES * j + t, 1), :]

    for jp in range(3):
        block = nn(h1[...], tiles_of(w, range(6 * jp, 6 * jp + 6))).astype(BF16)
        for k in range(6):
            t = 6 * jp + k
            tile = block[:, 128 * k:128 * (k + 1)]
            raw[t] = tile
            value = tile.astype(F32)
            conv = tap(0, t) * value + tap(1, t) * shifted(value, 1) + tap(2, t) * shifted(value, 2)
            mixed[t] = conv.astype(BF16)

    def both(value):
        zero = jnp.zeros_like(value)
        return jnp.concatenate([jnp.where(first, value, zero), jnp.where(first, zero, value)], axis=0)

    def pick(value):
        return jnp.where(first, value[:ROWS], value[ROWS:])

    def attend(p):
        query = both(mixed[p, ROWS:, :])
        key, value = mixed[PAIRS + p], mixed[2 * PAIRS + p]
        scores = nt(query, key) * 0.125 + jnp.concatenate([bias[...], bias[...]], axis=0)
        weights = jnp.exp(scores - jnp.max(scores, axis=-1, keepdims=True))
        exact = weights * (1.0 / jnp.sum(weights, axis=-1, keepdims=True))
        probs[p] = exact
        att[p] = pick(nn(exact.astype(BF16), value)).astype(BF16)

    for p in range(PAIRS):
        attend(p)

    attended = jnp.concatenate([att[p] for p in range(PAIRS)], axis=1)
    resid = tok[...].astype(F32) + nn(attended, tiles_of(w, range(18, 24)))
    normed_two, inverse_two = normalize(resid)
    h2[...] = (normed_two * gain_two).astype(BF16)
    h2t[...] = h2[...].T
    acc[...] = resid
    advance(phase[1], phase[1], phase[1])

    @pl.loop(0, 4)
    def _(jp):
        rect = jnp.maximum(nn(h2[...], columns(w, 1, jp)), 0.0)
        act[jp] = (rect * rect).astype(BF16)
        gup[jp] = rect.astype(BF16)

    for _ in range(6):
        advance(phase[2])
    place.drain()

    @pl.when(zl == 0)
    def _():
        place.copy(tok, tok, other, out_tokens, 0).wait_send()

    sibling = place.device(c=1 - c)
    across = [place.slot(3), place.slot(2), place.slot(4)]
    out_across = [place.outbox(w.at[part, 0]) for part in range(3)]
    every = slice(None)

    @pl.loop(0, 4)
    def _(jp):
        low = rows(w, jp)
        gup[jp] = (nt(cot[...], low) * 2.0 * gup[jp].astype(F32)).astype(BF16)
        acc[...] += nn(act[jp], low)
        put_rows(w, jp, tn(act[jp], cot[...]))
        some = (lax.div(jp, 2), slice(None), pl.ds(lax.rem(jp, 2) * 2, 2))
        place.send(w.at[(2, 1 - c) + some], from_core.at[(2,) + some], sibling, out_across[2], across[2] + jp)

    gh2[...] = jnp.zeros_like(gh2)

    def widen(jp):
        gh2[...] += nt(gup[jp], columns(w, 1, jp))
        put_columns(w, 1, jp, nn(h2t[...], gup[jp]))

        @pl.when(lax.rem(jp, 2) == 1 - c)
        def _():
            xl = lax.div(jp, 2)
            src, dst = w.at[1, 1 - c, :, :, :, :, xl], from_core.at[1, :, :, :, :, xl]
            place.send(src, dst, sibling, out_across[1], across[1] + xl)

    strips = [strip(sub) for sub in range(3)]

    def finish(part):
        def store(sub, total):
            sums[part, 16 * sub:16 * sub + 16, :] = total
        return store

    def finish_chunk(first, width):
        def store(sub, total):
            sums[0, 16 * sub:16 * sub + 16, first:first + width] = total
        return store

    def land(k):
        return [lands[12 * k + 4 * sub:12 * k + 4 * sub + 4] for sub in range(3)]

    def cross(k):
        cut = (1 - c,) + (every,) * 6 + (pl.ds(*CHUNKS[k]),)
        place.send(g0.at[cut], from_core.at[(0,) + cut[1:]], sibling, out_across[0], across[0] + k)

    up_ready = [((every,) * 4 + (xl,), across[1] + xl) for xl in range(2)]
    down_ready = [((jp // 2, every, pl.ds(jp % 2 * 2, 2)), across[2] + jp) for jp in range(4)]
    ups = scatter_phase(place, w, (1,), strips, up_ready, from_core.at[1], land(2), finish(1), True, LEAN_OUT[1])
    downs = scatter_phase(place, w, (2,), strips, down_ready, from_core.at[2], land(3), finish(2), True, LEAN_OUT[2])
    chunks = []
    for k, (start, width) in enumerate(CHUNKS):
        cut = (pl.ds(start, width),)
        came = [((every,) * 6 + cut, across[0] + k)]
        tails = [(pl.ds(16 * sub, 16),) + cut for sub in range(3)]
        chunks.append(scatter_phase(place, g0, (), tails, came, from_core.at[0], land(k), finish_chunk(start, width), k == 0, LEAN_OUT[0]))
    pl.loop(0, 2)(widen)
    advance(downs)
    pl.loop(2, 4)(widen)
    out[...] = acc[...].astype(BF16)
    grad_two = gh2[...]
    summed = jnp.sum(grad_two * normed_two, axis=0, keepdims=True)
    for r in range(6):
        gvec[0, 6 + r:7 + r, :] = summed[:, 128 * r:128 * (r + 1)]
    grad_resid = cot[...].astype(F32) + norm_back(grad_two * gain_two, normed_two, inverse_two)
    acc[...] = grad_resid
    gproj = grad_resid.astype(BF16)
    gback = nt(gproj, tiles_of(w, range(18, 24))).astype(BF16)
    for p in range(PAIRS):
        gatt[p] = gback[:, 128 * p:128 * (p + 1)]
    advance(ups)
    put_tiles(g0, range(18, 24), tn(attended, gproj))

    def attend_back(p):
        query = both(mixed[p, ROWS:, :])
        key, value = mixed[PAIRS + p], mixed[2 * PAIRS + p]
        grad = both(gatt[p])
        exact = probs[p]
        gvalue = tn(exact.astype(BF16), grad)
        gprobs = nt(grad, value)
        centred = gprobs - jnp.sum(gprobs * exact, axis=-1, keepdims=True)
        gscores = (exact * centred).astype(BF16)
        gquery = pick(nn(gscores, key)) * 0.125
        gkey = tn(gscores, query) * 0.125
        for k, tile in enumerate((jnp.concatenate([jnp.zeros_like(gquery), gquery], axis=0), gkey, gvalue)):
            t = PAIRS * k + p
            back = tap(0, t) * tile + tap(1, t) * shifted(tile, -1) + tap(2, t) * shifted(tile, -2)
            mixed[t] = back.astype(BF16)
            value_in = raw[t].astype(F32)
            for j in range(3):
                delayed = value_in if j == 0 else shifted(value_in, j)
                gvec[0, pl.ds(12 + TILES * j + t, 1), :] = jnp.sum(tile * delayed, axis=0, keepdims=True)

    def weigh(wanted):
        put_tiles(g0, wanted, nn(h1t[...], jnp.concatenate([mixed[t] for t in wanted], axis=1)))

    attend_back(0)
    attend_back(1)
    attend_back(2)
    attend_back(3)
    weigh(READY[6:16])
    cross(0)
    attend_back(4)
    attend_back(5)
    weigh(READY[16:24])
    cross(1)
    advance(downs)
    advance(chunks[0])

    out_back = place.outbox()

    def through_norm(half):
        here = pl.ds(half * ROWS, ROWS)
        grad_one = jnp.zeros((ROWS, D), F32)
        for jp in range(3):
            grad = jnp.concatenate([mixed[6 * jp + k, here, :] for k in range(6)], axis=1)
            grad_one = grad_one + nt(grad, tiles_of(w, range(6 * jp, 6 * jp + 6)))
        normed, inverse = normalize_half(half)
        return jnp.sum(grad_one * normed, axis=0, keepdims=True), norm_back(grad_one * gain_one, normed, inverse)

    total, back = through_norm(0)
    contrib[...] = back.astype(BF16)

    @pl.when(zl == 1)
    def _():
        place.send(contrib, got, other, out_back, back_slot)

    advance(ups)
    advance(chunks[1])
    gain, back = through_norm(1)
    acc[...] += back
    total = total + gain
    for r in range(6):
        gvec[0, r:r + 1, :] = total[:, 128 * r:128 * (r + 1)]
    small = sum_vectors(place, gvec, incoming)
    advance(small)
    advance(chunks[0], downs, ups, chunks[1])
    advance(small)
    advance(chunks[0], downs, ups, chunks[1])
    advance(small)
    advance(chunks[0], downs, ups)

    trades, trade_down = place.slot(2), place.slot()
    back_from, arrived = pile.at[0, pl.ds(0, 24)], from_peer
    out_trades, out_down = [place.outbox(from_peer.at[0, 0:7]) for _ in range(2)], place.outbox(back_from)

    def hand_back(k):
        for number in range(8):
            to_peer[k, number, 0:6, :] = sums[k, 6 * number:6 * number + 6, :]
        for d in range(1, 8):
            device, number = place.member(d)
            place.send(to_peer.at[k, number], arrived.at[k, mine], device, out_trades[k], trades + k)
        arrived[k, mine] = to_peer[k, mine]

    hand_back(1)
    place.send(sums.at[2, pl.ds(pl.multiple_of((1 - zl) * 24, 8), 24)], back_from, other, out_down, trade_down)
    advance(chunks[1], chunks[0])
    hand_back(0)
    advance(small, small, small)
    summed = gvec[4]
    gains = [jnp.concatenate([summed[r:r + 1] for r in range(6 * k, 6 * k + 6)], axis=1) for k in range(2)]
    tapped = [jnp.concatenate([summed[r:r + 1] for r in range(12 + TILES * j, 12 + TILES * j + TILES)], axis=1) for j in range(3)]
    gain_rows = jnp.concatenate(gains + [jnp.zeros((6, D), F32)], axis=0)
    tap_rows = jnp.concatenate(tapped + [jnp.zeros((5, 3 * D), F32)], axis=0)
    exactly = functools.partial(
        lax.dot_general,
        dimension_numbers=(((1,), (1,)), ((), ())),
        preferred_element_type=F32,
        precision=lax.Precision.HIGHEST,
    )
    gain_own = exactly(gain_rows, spread(place.index, 6, D))
    gga[...] = gain_own[0:1, 0:6]
    ggf[...] = gain_own[1:2, 0:6]
    gtap[...] = exactly(tap_rows, spread(place.index, 18, 3 * D))[0:3, 0:18]

    @pl.when(zl == 0)
    def _():
        place.arrive(got, back_slot)

    @pl.when(zl == 1)
    def _():
        got[...] = jnp.zeros_like(got)

    gtok[...] = (acc[...] + got[...].astype(F32)).astype(BF16)
    for k in range(2):
        place.arrive(arrived.at[k, 0:7], trades + k)
    place.arrive(back_from, trade_down)
    for number in range(8):
        for q in range(3):
            t = READY[8 * q + number]
            tile = arrived[0, number, 0:6, 128 * q:128 * (q + 1)]
            if t < 18:
                gq[:, 128 * t:128 * (t + 1)] = tile
            else:
                go[:, 128 * (t - 18):128 * (t - 17)] = tile
        gu[:, 384 * number:384 * (number + 1)] = arrived[1, number, 0:6, :]
    own = sums[2, pl.ds(pl.multiple_of(zl * 24, 8), 24), :]
    theirs = pile[0, 0:24, :]
    gd[:, 0:384] = jnp.where(zl == 0, own, theirs)
    gd[:, 384:768] = jnp.where(zl == 0, theirs, own)
    place.drain()

    @pl.when(zl == 1)
    def _():
        place.copy(contrib, contrib, other, out_back, 0).wait_send()


def kept(axes):
    grid = []
    for axis in "zyx":
        if axis not in axes:
            grid += {"z": [2, 2], "y": [4], "x": [2, 2]}[axis]
    return tuple(grid)


RESULTS = (
    ((ROWS, D), BF16),
    ((ROWS, D), BF16),
    ((6, 2304), F32),
    ((6, 768), F32),
    ((6, 3072), F32),
    ((24, 768), F32),
    ((1, 6), F32),
    ((1, 6), F32),
    ((3, 18), F32),
)


def layer(*args):
    vmem = pl.BlockSpec(memory_space=pltpu.VMEM)
    lands = []
    for k in range(4):
        for sub in range(3):
            order = BACK[sub]
            grids = [(2,) + HALVES[order[0]], (2,) + kept(order[:1]), (3,) + kept(order[:2]), (3,)]
            if k == 1:
                grids[:2] = [(1,), (3,) + kept(order[:1])]
            lands += [pltpu.VMEM(grid + (16, CHUNKS[k][1] if k < 2 else 384), BF16) for grid in grids]
    return pl.pallas_call(
        layer_kernel,
        out_shape=tuple(jax.ShapeDtypeStruct(*result) for result in RESULTS),
        in_specs=[vmem] * 9,
        out_specs=(vmem,) * 9,
        scratch_shapes=[
            pltpu.VMEM((3,) + GRID + BLOCK, BF16),
            pltpu.VMEM(GRID + BLOCK, BF16),
            pltpu.VMEM((D, EXT), BF16),
            pltpu.VMEM((D, ROWS), BF16),
            pltpu.VMEM((3,) + GRID[1:] + BLOCK, BF16),
            pltpu.VMEM((2, 8, 8, 384), F32),
            pltpu.VMEM((2, 8, 8, 384), F32),
            pltpu.VMEM((2, 56, 384), F32),
            pltpu.VMEM((24, 384), F32),
            pltpu.VMEM((48, 384), F32),
            pltpu.VMEM((8, 128), F32),
            pltpu.VMEM((4, 4, 8, 128), F32),
            pltpu.VMEM((8, 8, 128), F32),
            pltpu.VMEM((VEC, 128), F32),
            pltpu.VMEM((ROWS, D), BF16),
            pltpu.VMEM((EXT, D), BF16),
            pltpu.VMEM((TILES, EXT, 128), BF16),
            pltpu.VMEM((TILES, EXT, 128), BF16),
            pltpu.VMEM((ROWS, EXT), F32),
            pltpu.VMEM((PAIRS, EXT, EXT), F32),
            pltpu.VMEM((PAIRS, ROWS, 128), BF16),
            pltpu.VMEM((ROWS, D), BF16),
            pltpu.VMEM((4, ROWS, D), BF16),
            pltpu.VMEM((4, ROWS, D), BF16),
            pltpu.VMEM((ROWS, D), F32),
            pltpu.VMEM((PAIRS, ROWS, 128), BF16),
            pltpu.VMEM((ROWS, D), F32),
            pltpu.VMEM((ROWS, D), BF16),
            pltpu.VMEM((ROWS, D), BF16),
            pltpu.VMEM((5, VEC, 128), F32),
            pltpu.VMEM((4, 3, VEC, 128), F32),
            pltpu.VMEM((3,) + BLOCK, F32),
            *lands,
            pltpu.SemaphoreType.DMA((64,)),
            pltpu.SemaphoreType.DMA((120,)),
        ],
        compiler_params=pltpu.CompilerParams(collective_id=0, has_side_effects=True, vmem_limit_bytes=LIMIT),
    )(*args)


def copy_kernel(*refs):
    for source, target in zip(refs[:len(RESULTS)], refs[len(RESULTS):]):
        target[...] = source[...]


def copied(*args):
    vmem = pl.BlockSpec(memory_space=pltpu.VMEM)
    return pl.pallas_call(
        copy_kernel,
        out_shape=tuple(jax.ShapeDtypeStruct(*result) for result in RESULTS),
        in_specs=[vmem] * len(RESULTS),
        out_specs=(vmem,) * len(RESULTS),
    )(*args)


def per_device(tokens, w_qkv, w_out, w_up, w_down, gain_attn, gain_ffn, conv_taps, cotangent):
    results = copied(*layer(
        tokens, cotangent, w_qkv, w_out, w_up, w_down, gain_attn.reshape(1, 6), gain_ffn.reshape(1, 6), conv_taps
    ))
    return results[:6] + (results[6].reshape(6), results[7].reshape(6), results[8])


def solution(mesh):
    both = ("grp", "seq")
    row, one, column = P(both, None), P(both), P(None, both)
    return jax.shard_map(
        per_device,
        mesh=mesh,
        in_specs=(row, row, row, row, row, one, one, column, row),
        out_specs=(row, row, row, row, row, row, one, one, column),
        check_vma=False,
    )
```

time: 173 us -> 121 us (0.70)
  Pallas kernels: 172 us -> 120 us
    pallas_call x1, Pallas kernels: 33.3 us -> 2.22 us  [copied(): pl.pallas_call(copy_kernel, out_shape=tuple((jax.ShapeDtypeStruct(*result...]
    pallas_call x1, Pallas kernels: 139 us -> 118 us  [layer(): pl.pallas_call(layer_kernel, out_shape=tuple((jax.ShapeDtypeStruct(*resul...]
where the time goes in v3:
time: 121 us
  Pallas kernels  120 us (99%)
    pallas_call x1, Pallas kernels, layer(): pl.pallas_call(layer_kernel, out_shape=tuple((jax.ShapeDtypeStruct(*resul...  118 us

profile of v3, /device:TPU:1, one launch (start us, length us, event | category | flops | bytes accessed | tf_op | source)
XLA Modules:
  0.0 120.6 jit_solution(10325202845571059235)
XLA Ops:
  0.6 117.5 %shard_map.160 = (bf16[256,768]{1,0:T(8,128)(2,1)}, bf16[256,768]{1,0:T(8,128)(2,1)}, f32[6,2304]{1,0:T(8,128)}, f32[6,768]{1,0:T(8,128)}, f32[6,3072]{1,0:T(8,1...) custom-call(bf16[256,768]{1,0:T(8,128)(2,1)} %tok.1, bf16[256,768]{1,0:T(8,128)(2,1)} %cot.1, ...), custom_call_target="tpu_custom_call" | custom-call | tf_op jit(solution)/shard_map/pallas_call | solution.py:819
  118.2 2.2 %shard_map.161 = (bf16[256,768]{1,0:T(8,128)(2,1)}, bf16[256,768]{1,0:T(8,128)(2,1)}, f32[6,2304]{1,0:T(8,128)}, f32[6,768]{1,0:T(8,128)}, f32[6,3072]{1,0:T(8,1...) custom-call(bf16[256,768]{1,0:T(8,128)(2,1)} %get-tuple-element.27.refs_0_, ...), custom_call_target="tpu_custom_call" | custom-call | tf_op jit(solution)/shard_map/pallas_call | solution.py:872

commit v4 on v3

--- a/solution.py
+++ b/solution.py
@@ -472,6 +472,13 @@
             device, number = place.member(d)
             place.send(to_peer.at[k, number], from_peer.at[k, mine], device, out_trades[k], trades + k)
 
+    def send_tokens(k):
+        piece = pl.ds(64 * k, 64)
+
+        @pl.when(zl == 0)
+        def _():
+            place.send(tok.at[piece], prev.at[piece], other, out_tokens, token_slot)
+
     trade(0)
     trade(1)
     place.send(down_s, down.at[pl.ds(pl.multiple_of(zl * 24, 8), 24)], other, out_down, trade_down)
@@ -483,6 +490,7 @@
     def normalize_half(half):
         return normalize((prev if half == 0 else tok)[...].astype(F32))
 
+    send_tokens(0)
     place.arrive(down_s, trade_down)
     at = (c, lax.div(place.z, 2), zl, place.y, lax.div(place.x, 2), lax.rem(place.x, 2))
     for k in range(2):
@@ -493,13 +501,10 @@
     w[(2,) + at] = down[...].astype(BF16)
     phase = [gather_phase(place, w, part, LEAN_IN[part]) for part in range(3)]
     advance(vectors)
-    for _ in range(3):
+    for k in range(3):
         advance(*phase)
+        send_tokens(k + 1)
         advance(vectors)
-
-    @pl.when(zl == 0)
-    def _():
-        place.send(tok, prev, other, out_tokens, token_slot)
 
     advance(*phase)
 
@@ -522,8 +527,7 @@
     bias[...] = jnp.where(behind <= row, 0.0, -1e30)
     first = lax.broadcasted_iota(jnp.int32, (ROWS, 128), 1) < 64
     gvec[0] = jnp.zeros((VEC, 128), F32)
-    advance(*phase)
-    advance(phase[0])
+    advance(phase[0], phase[0])
 
     def tap(j, t):
         return vec[pl.ds(12 + TILES * j + t, 1), :]
@@ -554,8 +558,11 @@
         probs[p] = exact
         att[p] = pick(nn(exact.astype(BF16), value)).astype(BF16)
 
+    advance(phase[1])
     for p in range(PAIRS):
         attend(p)
+        if p == 0:
+            advance(phase[2])
 
     attended = jnp.concatenate([att[p] for p in range(PAIRS)], axis=1)
     resid = tok[...].astype(F32) + nn(attended, tiles_of(w, range(18, 24)))
@@ -648,7 +655,6 @@
     gback = nt(gproj, tiles_of(w, range(18, 24))).astype(BF16)
     for p in range(PAIRS):
         gatt[p] = gback[:, 128 * p:128 * (p + 1)]
-    advance(ups)
     put_tiles(g0, range(18, 24), tn(attended, gproj))
 
     def attend_back(p):
@@ -675,18 +681,18 @@
         put_tiles(g0, wanted, nn(h1t[...], jnp.concatenate([mixed[t] for t in wanted], axis=1)))
 
     attend_back(0)
+    advance(ups)
     attend_back(1)
     attend_back(2)
     attend_back(3)
     weigh(READY[6:16])
     cross(0)
+    advance(downs)
     attend_back(4)
     attend_back(5)
+    advance(chunks[0])
     weigh(READY[16:24])
     cross(1)
-    advance(downs)
-    advance(chunks[0])
-
     out_back = place.outbox()
 
     def through_norm(half):
@@ -698,15 +704,17 @@
         normed, inverse = normalize_half(half)
         return jnp.sum(grad_one * normed, axis=0, keepdims=True), norm_back(grad_one * gain_one, normed, inverse)
 
+    def send_back(k):
+        piece = pl.ds(64 * k, 64)
+
+        @pl.when(zl == 1)
+        def _():
+            place.send(contrib.at[piece], got.at[piece], other, out_back, back_slot)
+
+    advance(ups)
     total, back = through_norm(0)
     contrib[...] = back.astype(BF16)
-
-    @pl.when(zl == 1)
-    def _():
-        place.send(contrib, got, other, out_back, back_slot)
-
-    advance(ups)
-    advance(chunks[1])
+    send_back(0)
     gain, back = through_norm(1)
     acc[...] += back
     total = total + gain
@@ -714,10 +722,15 @@
         gvec[0, r:r + 1, :] = total[:, 128 * r:128 * (r + 1)]
     small = sum_vectors(place, gvec, incoming)
     advance(small)
+    advance(chunks[1])
+    advance(small)
+    send_back(1)
     advance(chunks[0], downs, ups, chunks[1])
     advance(small)
+    send_back(2)
     advance(chunks[0], downs, ups, chunks[1])
     advance(small)
+    send_back(3)
     advance(chunks[0], downs, ups)
 
     trades, trade_down = place.slot(2), place.slot()
@@ -736,7 +749,7 @@
     place.send(sums.at[2, pl.ds(pl.multiple_of((1 - zl) * 24, 8), 24)], back_from, other, out_down, trade_down)
     advance(chunks[1], chunks[0])
     hand_back(0)
-    advance(small, small, small)
+    advance(small, small)
     summed = gvec[4]
     gains = [jnp.concatenate([summed[r:r + 1] for r in range(6 * k, 6 * k + 6)], axis=1) for k in range(2)]
     tapped = [jnp.concatenate([summed[r:r + 1] for r in range(12 + TILES * j, 12 + TILES * j + TILES)], axis=1) for j in range(3)]

time: 121 us -> 110 us (0.909)
  Pallas kernels: 120 us -> 109 us
    pallas_call x1, Pallas kernels: 118 us -> 107 us  [layer(): pl.pallas_call(layer_kernel, out_shape=tuple((jax.ShapeDtypeStruct(*resul...]
where the time goes in v4:
time: 110 us
  Pallas kernels  109 us (99%)
    pallas_call x1, Pallas kernels, layer(): pl.pallas_call(layer_kernel, out_shape=tuple((jax.ShapeDtypeStruct(*resul...  107 us
    pallas_call x1, Pallas kernels, copied(): pl.pallas_call(copy_kernel, out_shape=tuple((jax.ShapeDtypeStruct(*result...  2.22 us

profile of v4, /device:TPU:1, one launch (start us, length us, event | category | flops | bytes accessed | tf_op | source)
XLA Modules:
  0.0 110.2 jit_solution(17337255081233074891)
XLA Ops:
  0.6 107.2 %shard_map.160 = (bf16[256,768]{1,0:T(8,128)(2,1)}, bf16[256,768]{1,0:T(8,128)(2,1)}, f32[6,2304]{1,0:T(8,128)}, f32[6,768]{1,0:T(8,128)}, f32[6,3072]{1,0:T(8,1...) custom-call(bf16[256,768]{1,0:T(8,128)(2,1)} %tok.1, bf16[256,768]{1,0:T(8,128)(2,1)} %cot.1, ...), custom_call_target="tpu_custom_call" | custom-call | tf_op jit(solution)/shard_map/pallas_call | solution.py:832
  107.9 2.2 %shard_map.161 = (bf16[256,768]{1,0:T(8,128)(2,1)}, bf16[256,768]{1,0:T(8,128)(2,1)}, f32[6,2304]{1,0:T(8,128)}, f32[6,768]{1,0:T(8,128)}, f32[6,3072]{1,0:T(8,1...) custom-call(bf16[256,768]{1,0:T(8,128)(2,1)} %get-tuple-element.27.refs_0_, ...), custom_call_target="tpu_custom_call" | custom-call | tf_op jit(solution)/shard_map/pallas_call | solution.py:885

commit v5 on v4

--- a/solution.py
+++ b/solution.py
@@ -386,7 +386,7 @@
 def put_tiles(g, wanted, value):
     low = value.astype(BF16)
     for k, t in enumerate(wanted):
-        g[tile_at(t)] = low[:, 128 * k:128 * (k + 1)].reshape(2, 4, 2, 48, 128)
+        g[(2,) + tile_at(t)] = low[:, 128 * k:128 * (k + 1)].reshape(2, 4, 2, 48, 128)
 
 
 def put_columns(ref, part, jp, value):
@@ -413,7 +413,7 @@
     low = value.astype(BF16)
     for zl in range(2):
         for k, (y, xh, xl, c) in enumerate(row_pieces()):
-            ref[2, c, zh, zl, y0 + y, xh, xl] = low[48 * k:48 * k + 48, zl * 384:(zl + 1) * 384]
+            ref[c, zh, zl, y0 + y, xh, xl] = low[48 * k:48 * k + 48, zl * 384:(zl + 1) * 384]
 
 
 def normalize(values):
@@ -501,12 +501,15 @@
     w[(2,) + at] = down[...].astype(BF16)
     phase = [gather_phase(place, w, part, LEAN_IN[part]) for part in range(3)]
     advance(vectors)
-    for k in range(3):
+    for k in range(2):
         advance(*phase)
         send_tokens(k + 1)
         advance(vectors)
-
-    advance(*phase)
+    advance(phase[0], phase[1])
+    send_tokens(3)
+    advance(vectors)
+
+    advance(phase[0], phase[2], phase[1])
 
     @pl.when(zl == 1)
     def _():
@@ -527,7 +530,7 @@
     bias[...] = jnp.where(behind <= row, 0.0, -1e30)
     first = lax.broadcasted_iota(jnp.int32, (ROWS, 128), 1) < 64
     gvec[0] = jnp.zeros((VEC, 128), F32)
-    advance(phase[0], phase[0])
+    advance(phase[0], phase[2], phase[0])
 
     def tap(j, t):
         return vec[pl.ds(12 + TILES * j + t, 1), :]
@@ -571,35 +574,68 @@
     h2t[...] = h2[...].T
     acc[...] = resid
     advance(phase[1], phase[1], phase[1])
+    inward, place.owed = place.owed, []
+    sibling = place.device(c=1 - c)
+    across = [place.slot(3), place.slot(2), place.slot(4)]
+    out_across = [place.outbox(w.at[part, 0]) for part in range(3)]
+    every = slice(None)
+    strips = [strip(sub) for sub in range(3)]
+
+    def finish(part):
+        def store(sub, total):
+            sums[part, 16 * sub:16 * sub + 16, :] = total
+        return store
+
+    def finish_chunk(first, width):
+        def store(sub, total):
+            sums[0, 16 * sub:16 * sub + 16, first:first + width] = total
+        return store
+
+    def land(k):
+        return [lands[12 * k + 4 * sub:12 * k + 4 * sub + 4] for sub in range(3)]
+
+    def cross(k):
+        cut = (1 - c,) + (every,) * 6 + (pl.ds(*CHUNKS[k]),)
+        place.send(w.at[(2,) + cut], from_core.at[(0,) + cut[1:]], sibling, out_across[0], across[0] + k)
+
+    up_ready = [((every,) * 4 + (xl,), across[1] + xl) for xl in range(2)]
+    down_ready = [((jp // 2, every, pl.ds(jp % 2 * 2, 2)), across[2] + jp) for jp in range(4)]
+    ups = scatter_phase(place, w, (1,), strips, up_ready, from_core.at[1], land(2), finish(1), True, LEAN_OUT[1])
+    downs = scatter_phase(place, g0, (), strips, down_ready, from_core.at[2], land(3), finish(2), True, LEAN_OUT[2])
+    chunks = []
+    for k, (start, width) in enumerate(CHUNKS):
+        cut = (pl.ds(start, width),)
+        came = [((every,) * 6 + cut, across[0] + k)]
+        tails = [(pl.ds(16 * sub, 16),) + cut for sub in range(3)]
+        chunks.append(scatter_phase(place, w, (2,), tails, came, from_core.at[0], land(k), finish_chunk(start, width), k == 0, LEAN_OUT[0]))
 
     @pl.loop(0, 4)
     def _(jp):
         rect = jnp.maximum(nn(h2[...], columns(w, 1, jp)), 0.0)
         act[jp] = (rect * rect).astype(BF16)
         gup[jp] = rect.astype(BF16)
+        put_rows(g0, jp, tn(act[jp], cot[...]))
+        some = (lax.div(jp, 2), slice(None), pl.ds(lax.rem(jp, 2) * 2, 2))
+        place.send(g0.at[(1 - c,) + some], from_core.at[(2,) + some], sibling, out_across[2], across[2] + jp)
 
     for _ in range(6):
         advance(phase[2])
+    place.owed, outward = inward, place.owed
     place.drain()
+    place.owed = outward
 
     @pl.when(zl == 0)
     def _():
         place.copy(tok, tok, other, out_tokens, 0).wait_send()
 
-    sibling = place.device(c=1 - c)
-    across = [place.slot(3), place.slot(2), place.slot(4)]
-    out_across = [place.outbox(w.at[part, 0]) for part in range(3)]
-    every = slice(None)
-
-    @pl.loop(0, 4)
-    def _(jp):
+    def narrow(jp):
         low = rows(w, jp)
         gup[jp] = (nt(cot[...], low) * 2.0 * gup[jp].astype(F32)).astype(BF16)
         acc[...] += nn(act[jp], low)
-        put_rows(w, jp, tn(act[jp], cot[...]))
-        some = (lax.div(jp, 2), slice(None), pl.ds(lax.rem(jp, 2) * 2, 2))
-        place.send(w.at[(2, 1 - c) + some], from_core.at[(2,) + some], sibling, out_across[2], across[2] + jp)
-
+
+    pl.loop(0, 2)(narrow)
+    advance(downs)
+    pl.loop(2, 4)(narrow)
     gh2[...] = jnp.zeros_like(gh2)
 
     def widen(jp):
@@ -612,38 +648,7 @@
             src, dst = w.at[1, 1 - c, :, :, :, :, xl], from_core.at[1, :, :, :, :, xl]
             place.send(src, dst, sibling, out_across[1], across[1] + xl)
 
-    strips = [strip(sub) for sub in range(3)]
-
-    def finish(part):
-        def store(sub, total):
-            sums[part, 16 * sub:16 * sub + 16, :] = total
-        return store
-
-    def finish_chunk(first, width):
-        def store(sub, total):
-            sums[0, 16 * sub:16 * sub + 16, first:first + width] = total
-        return store
-
-    def land(k):
-        return [lands[12 * k + 4 * sub:12 * k + 4 * sub + 4] for sub in range(3)]
-
-    def cross(k):
-        cut = (1 - c,) + (every,) * 6 + (pl.ds(*CHUNKS[k]),)
-        place.send(g0.at[cut], from_core.at[(0,) + cut[1:]], sibling, out_across[0], across[0] + k)
-
-    up_ready = [((every,) * 4 + (xl,), across[1] + xl) for xl in range(2)]
-    down_ready = [((jp // 2, every, pl.ds(jp % 2 * 2, 2)), across[2] + jp) for jp in range(4)]
-    ups = scatter_phase(place, w, (1,), strips, up_ready, from_core.at[1], land(2), finish(1), True, LEAN_OUT[1])
-    downs = scatter_phase(place, w, (2,), strips, down_ready, from_core.at[2], land(3), finish(2), True, LEAN_OUT[2])
-    chunks = []
-    for k, (start, width) in enumerate(CHUNKS):
-        cut = (pl.ds(start, width),)
-        came = [((every,) * 6 + cut, across[0] + k)]
-        tails = [(pl.ds(16 * sub, 16),) + cut for sub in range(3)]
-        chunks.append(scatter_phase(place, g0, (), tails, came, from_core.at[0], land(k), finish_chunk(start, width), k == 0, LEAN_OUT[0]))
-    pl.loop(0, 2)(widen)
-    advance(downs)
-    pl.loop(2, 4)(widen)
+    pl.loop(0, 4)(widen)
     out[...] = acc[...].astype(BF16)
     grad_two = gh2[...]
     summed = jnp.sum(grad_two * normed_two, axis=0, keepdims=True)
@@ -655,7 +660,7 @@
     gback = nt(gproj, tiles_of(w, range(18, 24))).astype(BF16)
     for p in range(PAIRS):
         gatt[p] = gback[:, 128 * p:128 * (p + 1)]
-    put_tiles(g0, range(18, 24), tn(attended, gproj))
+    put_tiles(w, range(18, 24), tn(attended, gproj))
 
     def attend_back(p):
         query = both(mixed[p, ROWS:, :])
@@ -678,7 +683,7 @@
                 gvec[0, pl.ds(12 + TILES * j + t, 1), :] = jnp.sum(tile * delayed, axis=0, keepdims=True)
 
     def weigh(wanted):
-        put_tiles(g0, wanted, nn(h1t[...], jnp.concatenate([mixed[t] for t in wanted], axis=1)))
+        put_tiles(w, wanted, nn(h1t[...], jnp.concatenate([mixed[t] for t in wanted], axis=1)))
 
     attend_back(0)
     advance(ups)
@@ -868,8 +873,8 @@
             pltpu.VMEM((4, 3, VEC, 128), F32),
             pltpu.VMEM((3,) + BLOCK, F32),
             *lands,
-            pltpu.SemaphoreType.DMA((64,)),
-            pltpu.SemaphoreType.DMA((120,)),
+            pltpu.SemaphoreType.DMA((43,)),
+            pltpu.SemaphoreType.DMA((93,)),
         ],
         compiler_params=pltpu.CompilerParams(collective_id=0, has_side_effects=True, vmem_limit_bytes=LIMIT),
     )(*args)

time: 110 us -> 110 us (level)
  no operation moved by 1% of the time
where the time goes in v5:
time: 110 us
  Pallas kernels  109 us (99%)
    pallas_call x1, Pallas kernels, layer(): pl.pallas_call(layer_kernel, out_shape=tuple((jax.ShapeDtypeStruct(*resul...  107 us
    pallas_call x1, Pallas kernels, copied(): pl.pallas_call(copy_kernel, out_shape=tuple((jax.ShapeDtypeStruct(*result...  2.22 us

profile of v5, /device:TPU:1, one launch (start us, length us, event | category | flops | bytes accessed | tf_op | source)
XLA Modules:
  0.0 110.2 jit_solution(11453733317443344183)
XLA Ops:
  0.6 107.2 %shard_map.160 = (bf16[256,768]{1,0:T(8,128)(2,1)}, bf16[256,768]{1,0:T(8,128)(2,1)}, f32[6,2304]{1,0:T(8,128)}, f32[6,768]{1,0:T(8,128)}, f32[6,3072]{1,0:T(8,1...) custom-call(bf16[256,768]{1,0:T(8,128)(2,1)} %tok.1, bf16[256,768]{1,0:T(8,128)(2,1)} %cot.1, ...), custom_call_target="tpu_custom_call" | custom-call | tf_op jit(solution)/shard_map/pallas_call | solution.py:837
  107.9 2.2 %shard_map.161 = (bf16[256,768]{1,0:T(8,128)(2,1)}, bf16[256,768]{1,0:T(8,128)(2,1)}, f32[6,2304]{1,0:T(8,128)}, f32[6,768]{1,0:T(8,128)}, f32[6,3072]{1,0:T(8,1...) custom-call(bf16[256,768]{1,0:T(8,128)(2,1)} %get-tuple-element.27.refs_0_, ...), custom_call_target="tpu_custom_call" | custom-call | tf_op jit(solution)/shard_map/pallas_call | solution.py:890

commit v6 on v5

--- a/solution.py
+++ b/solution.py
@@ -729,14 +729,17 @@
     advance(small)
     advance(chunks[1])
     advance(small)
+    advance(chunks[0])
     send_back(1)
-    advance(chunks[0], downs, ups, chunks[1])
+    advance(downs, ups, chunks[1])
     advance(small)
+    advance(chunks[0])
     send_back(2)
-    advance(chunks[0], downs, ups, chunks[1])
+    advance(downs, ups, chunks[1])
     advance(small)
+    advance(chunks[0])
     send_back(3)
-    advance(chunks[0], downs, ups)
+    advance(downs, ups)
 
     trades, trade_down = place.slot(2), place.slot()
     back_from, arrived = pile.at[0, pl.ds(0, 24)], from_peer

time: 110 us -> 110 us (level)
  no operation moved by 1% of the time
where the time goes in v6:
time: 110 us
  Pallas kernels  109 us (99%)
    pallas_call x1, Pallas kernels, layer(): pl.pallas_call(layer_kernel, out_shape=tuple((jax.ShapeDtypeStruct(*resul...  107 us
    pallas_call x1, Pallas kernels, copied(): pl.pallas_call(copy_kernel, out_shape=tuple((jax.ShapeDtypeStruct(*result...  2.22 us

profile of v6, /device:TPU:1, one launch (start us, length us, event | category | flops | bytes accessed | tf_op | source)
XLA Modules:
  0.0 110.1 jit_solution(3473245171204566998)
XLA Ops:
  0.6 107.1 %shard_map.160 = (bf16[256,768]{1,0:T(8,128)(2,1)}, bf16[256,768]{1,0:T(8,128)(2,1)}, f32[6,2304]{1,0:T(8,128)}, f32[6,768]{1,0:T(8,128)}, f32[6,3072]{1,0:T(8,1...) custom-call(bf16[256,768]{1,0:T(8,128)(2,1)} %tok.1, bf16[256,768]{1,0:T(8,128)(2,1)} %cot.1, ...), custom_call_target="tpu_custom_call" | custom-call | tf_op jit(solution)/shard_map/pallas_call | solution.py:840
  107.7 2.2 %shard_map.161 = (bf16[256,768]{1,0:T(8,128)(2,1)}, bf16[256,768]{1,0:T(8,128)(2,1)}, f32[6,2304]{1,0:T(8,128)}, f32[6,768]{1,0:T(8,128)}, f32[6,3072]{1,0:T(8,1...) custom-call(bf16[256,768]{1,0:T(8,128)(2,1)} %get-tuple-element.27.refs_0_, ...), custom_call_target="tpu_custom_call" | custom-call | tf_op jit(solution)/shard_map/pallas_call | solution.py:893
